TPU v7x, 32 devices: a whole 2x2x4 slice. The times are simulated.
32 devices in a mesh: gx: 8 (over z, x), gy: 4 (over y, core).
Axes of the slice: x: 2, y: 2, z: 4, core: 2. Of those that a mesh axis runs over, the one named last changes fastest.
Arguments:
- queries: bfloat16 [128, 128, 128], P('gx', 'gy'), may hold values from -6 to 6
- keys: bfloat16 [128, 128, 128], P('gx', 'gy'), may hold values from -6 to 6
- values: bfloat16 [128, 128, 128], P('gx', 'gy'), may hold values from -6 to 6
- out_attn: bfloat16 [128, 128, 128], P('gx', 'gy'), may hold values from -6 to 6
- out_grad: bfloat16 [128, 128, 128], P('gx', 'gy'), may hold values from -6 to 6
- log_norm: bfloat16 [4, 128, 128], P(None, 'gx', 'gy'), may hold values from 3 to 4
- neighbour_blocks: int32 [8, 16, 3], P('gx', 'gy'), may hold values from 0 to 15, as said below
- stencil: float32 [5, 128], replicated, may hold values from -3 to 3
Outputs:
- query_grad: bfloat16 [128, 128, 128], P('gx', 'gy')
- key_grad: bfloat16 [128, 128, 128], P('gx', 'gy')
- value_grad: bfloat16 [128, 128, 128], P('gx', 'gy')
- stencil_grad: float32 [5, 128], replicated
Inputs may be any that keep to these rules, and one draw needn't show every extreme that they name: `neighbour_blocks`: among the entries of the 4 row blocks of one tile, at most 3 name blocks of any one tile of the strip (the tile of block c is c // 4), and exactly 3 do for some tile.
All inputs are finite; a program needn't handle non-finite values.
Results may differ from a plain program's by a relative error of at most 0.0054.
Values may be sent and summed in bfloat16 or wider, within the bound.
A program may use at most 64 MiB of HBM per device.

v0:
```python
import math

import jax
import jax.numpy as jnp
from jax import lax
from jax.sharding import PartitionSpec as P

BLOCK = 128
HEADS = 4


def with_halo(block, sides, width):
    for axis, dim in sides:
        count = lax.axis_size(axis)
        forward = [(i, i + 1) for i in range(count - 1)]
        forward.append((count - 1, 0))
        backward = [(target, source) for source, target in forward]
        low = lax.ppermute(
            lax.slice_in_dim(block, block.shape[dim] - width, None, axis=dim), axis, forward
        )
        high = lax.ppermute(lax.slice_in_dim(block, 0, width, axis=dim), axis, backward)
        block = jnp.concatenate([low, block, high], axis=dim)
    return block


def tile_grads(row_pack, stat_pack, key_pack):
    item_count = row_pack.shape[0]
    block_rows = row_pack.shape[2]
    features = row_pack.shape[3]
    head_width = features // HEADS
    softmax_scale = 1.0 / math.sqrt(head_width)
    row_heads = row_pack.reshape(item_count, 2, block_rows, HEADS, head_width).transpose(
        0, 1, 3, 4, 2
    )
    key_heads_all = key_pack.reshape(item_count, 2, block_rows, HEADS, head_width).transpose(
        0, 1, 3, 4, 2
    )
    query_heads = row_heads[:, 0]
    grad_heads = row_heads[:, 1]
    key_heads = key_heads_all[:, 0]
    value_heads = key_heads_all[:, 1]
    log_part = stat_pack[:, 0].astype(jnp.float32)
    delta_part = stat_pack[:, 1].astype(jnp.float32)
    scores = (
        jnp.einsum("shdq,shdk->shqk", query_heads, key_heads, preferred_element_type=jnp.float32)
        * softmax_scale
    )
    weights = jnp.exp(scores - log_part[..., None])
    weight_grad = jnp.einsum(
        "shdq,shdk->shqk", grad_heads, value_heads, preferred_element_type=jnp.float32
    )
    score_grad = weights * (weight_grad - delta_part[..., None])
    weights_low = weights.astype(jnp.bfloat16)
    score_low = score_grad.astype(jnp.bfloat16)
    value_part = jnp.einsum(
        "shqk,shdq->shdk", weights_low, grad_heads, preferred_element_type=jnp.float32
    )
    key_part = (
        jnp.einsum("shqk,shdq->shdk", score_low, query_heads, preferred_element_type=jnp.float32)
        * softmax_scale
    )
    query_part = (
        jnp.einsum("shqk,shdk->shdq", score_low, key_heads, preferred_element_type=jnp.float32)
        * softmax_scale
    )

    def points_last(part):
        return part.reshape(item_count, features, block_rows).transpose(0, 2, 1)

    return (points_last(query_part), points_last(key_part), points_last(value_part))


def per_device(queries, keys, values, out_attn, out_grad, log_norm, neighbour_blocks, stencil):
    tile_x, tile_y, features = queries.shape
    row_blocks = tile_x * tile_y // BLOCK
    head_width = features // HEADS
    listed = neighbour_blocks.shape[2]
    group_size = lax.axis_size("gy")
    pair_count = row_blocks * listed
    capacity = max(2, (pair_count + group_size - 1) // group_size)
    slot_count = group_size * capacity
    query_blocks = queries.reshape(row_blocks, BLOCK, features)
    key_blocks = keys.reshape(row_blocks, BLOCK, features)
    value_blocks = values.reshape(row_blocks, BLOCK, features)
    grad_blocks = out_grad.reshape(row_blocks, BLOCK, features)
    products = out_grad.astype(jnp.float32) * out_attn.astype(jnp.float32)
    delta = products.reshape(row_blocks, BLOCK, HEADS, head_width).sum(-1).astype(jnp.bfloat16)
    delta = delta.transpose(0, 2, 1)
    norm_blocks = log_norm.reshape(HEADS, row_blocks, BLOCK).transpose(1, 0, 2)
    stat_blocks = jnp.stack([norm_blocks, delta], 1)
    row_pack = jnp.stack([query_blocks, grad_blocks], 1)
    key_pack = jnp.stack([key_blocks, value_blocks], 1)
    diag_query, diag_key, diag_value = tile_grads(row_pack, stat_blocks, key_pack)
    columns = neighbour_blocks.reshape(pair_count)
    owners = columns // row_blocks
    inner = columns % row_blocks
    order = jnp.arange(pair_count, dtype=jnp.int32)
    before = (owners[:, None] == owners[None, :]) & (order[None, :] < order[:, None])
    rank = jnp.sum(before.astype(jnp.int32), 1)
    slot_of = owners * capacity + rank
    placed = (jnp.arange(slot_count, dtype=jnp.int32)[:, None] == slot_of[None, :]).astype(
        jnp.float32
    )
    source_rows = (
        (order // listed)[:, None] == jnp.arange(row_blocks, dtype=jnp.int32)[None, :]
    ).astype(jnp.float32)
    picker = jnp.dot(placed, source_rows, precision=lax.Precision.HIGHEST)
    picker_low = picker.astype(jnp.bfloat16)
    send_rows = jnp.dot(
        picker_low, row_pack.reshape(row_blocks, -1), preferred_element_type=jnp.float32
    )
    send_rows = send_rows.astype(jnp.bfloat16).reshape(group_size, capacity, 2, BLOCK, features)
    send_stats = jnp.dot(
        picker_low, stat_blocks.reshape(row_blocks, -1), preferred_element_type=jnp.float32
    )
    send_stats = send_stats.astype(jnp.bfloat16).reshape(group_size, capacity, 2, HEADS, BLOCK)
    send_ids = jnp.dot(placed, (inner + 1).astype(jnp.float32), precision=lax.Precision.HIGHEST)
    send_ids = send_ids.astype(jnp.bfloat16).reshape(group_size, capacity)
    rows_in = lax.all_to_all(send_rows, "gy", split_axis=0, concat_axis=0, tiled=True)
    stats_in = lax.all_to_all(send_stats, "gy", split_axis=0, concat_axis=0, tiled=True)
    ids_in = lax.all_to_all(send_ids, "gy", split_axis=0, concat_axis=0, tiled=True)
    item_count = rows_in.shape[1]
    total_items = group_size * item_count
    wanted = ids_in.astype(jnp.float32).astype(jnp.int32) - 1
    chooser = (wanted[..., None] == jnp.arange(row_blocks, dtype=jnp.int32)).astype(jnp.bfloat16)
    keys_in = jnp.dot(
        chooser.reshape(-1, row_blocks),
        key_pack.reshape(row_blocks, -1),
        preferred_element_type=jnp.float32,
    )
    keys_in = keys_in.astype(jnp.bfloat16).reshape(total_items, 2, BLOCK, features)
    query_part, key_part, value_part = tile_grads(
        rows_in.reshape(total_items, 2, BLOCK, features),
        stats_in.reshape(total_items, 2, HEADS, BLOCK),
        keys_in,
    )
    query_part = query_part.reshape(group_size, item_count, BLOCK, features)
    key_part = key_part.reshape(group_size, item_count, BLOCK, features)
    value_part = value_part.reshape(group_size, item_count, BLOCK, features)
    returned = lax.all_to_all(query_part, "gy", split_axis=0, concat_axis=0, tiled=True)
    returned, pieces, ids_in = (returned, jnp.stack([key_part, value_part], 2), ids_in)
    query_sum = diag_query + jnp.einsum(
        "sr,sbf->rbf",
        picker,
        returned.reshape(slot_count, BLOCK, features),
        precision=lax.Precision.HIGHEST,
    )
    arrived = ids_in.reshape(slot_count).astype(jnp.float32).astype(jnp.int32) - 1
    owned = (arrived[:, None] == jnp.arange(row_blocks, dtype=jnp.int32)[None, :]).astype(
        jnp.float32
    )
    key_value_sum = jnp.einsum(
        "sr,sxbf->rxbf",
        owned,
        pieces.reshape(slot_count, 2, BLOCK, features),
        precision=lax.Precision.HIGHEST,
    )
    key_total = diag_key + key_value_sum[:, 0]
    value_total = diag_value + key_value_sum[:, 1]
    rim = with_halo(out_grad, (("gx", 0), ("gy", 1)), 1)
    moved = [
        out_grad.astype(jnp.float32),
        rim[2:, 1:-1].astype(jnp.float32),
        rim[:-2, 1:-1].astype(jnp.float32),
        rim[1:-1, 2:].astype(jnp.float32),
        rim[1:-1, :-2].astype(jnp.float32),
    ]
    value_float = values.astype(jnp.float32)
    stencil_term = stencil[0] * moved[0]
    for index in range(1, 5):
        stencil_term = stencil_term + stencil[index] * moved[index]
    partial_rows = jnp.stack(
        [jnp.sum(moved[index] * value_float, axis=(0, 1)) for index in range(5)]
    )
    summed = lax.psum(partial_rows, ("gx", "gy"))
    point_count = tile_x * tile_y * lax.axis_size("gx") * group_size
    stencil_grad = summed / math.sqrt(point_count)
    query_grad = query_sum.reshape(tile_x, tile_y, features).astype(jnp.bfloat16)
    key_grad = key_total.reshape(tile_x, tile_y, features).astype(jnp.bfloat16)
    value_grad = (value_total.reshape(tile_x, tile_y, features) + stencil_term).astype(jnp.bfloat16)
    return (query_grad, key_grad, value_grad, stencil_grad)


def solution(mesh):
    placed = (
        P("gx", "gy", None),
        P("gx", "gy", None),
        P("gx", "gy", None),
        P("gx", "gy", None),
        P("gx", "gy", None),
        P(None, "gx", "gy"),
        P("gx", "gy", None),
        P(),
    )
    return jax.shard_map(
        per_device,
        mesh=mesh,
        in_specs=placed,
        out_specs=(P("gx", "gy", None), P("gx", "gy", None), P("gx", "gy", None), P()),
        check_vma=False,
    )
```

profile of v0, /device:TPU:0, one launch (start us, length us, event | category | flops | bytes accessed | tf_op | source)
XLA Modules:
  0.0 125.4 jit_solution(12477737306179112979)
XLA Ops:
  0.7 0.8 copy.93
  2.6 4.2 %all-to-all-start = ((bf16[4,1,3]{2,1,0:T(2,128)(2,1)}), bf16[4,1,3]{2,1,0:T(2,128)(2,1)S(1)}, u32[]{:S(2)}, u32[]{:S(2)}) async-start(bf16[4,1,3]{2,1,0:T(2,128)(2,1)} %all_to_all.20), calls=%async_computation | async-start | bytes 4096 | tf_op jit(solution)/shard_map/all_to_all | solution.py:121
  7.6 5.0 %collective-permute-start = (bf16[1,32,128]{2,1,0:T(8,128)(2,1)S(1)}, bf16[1,32,128]{2,1,0:T(8,128)(2,1)S(1)}, u32[]{:S(2)}, u32[]{:S(2)}) collective-permute-start(bf16[1,32,128]{2,1,0:T(8,128)(2,1)S(1)} %get-tuple-element.17), channel_id=1, source_target_pairs={{4,0},{8,4},{12,8},{16,12},{20,16},{24,20},{28,24},{0,28},{5,1},{9... | collective-permute-start | bytes 24584 | tf_op jit(solution)/shard_map/ppermute | solution.py:21
  12.5 1.1 reshape.238
  13.9 1.5 %slice_bitcast_fusion.30 = (f32[128]{0:T(128)}, f32[128]{0:T(128)}, f32[128]{0:T(128)}, f32[128]{0:T(128)}, f32[128]{0:T(128)}) fusion(f32[5,128]{1,0:T(8,128)} %param.15), kind=kLoop, calls=%fused_computation.120 | loop fusion | bytes 5120 | tf_op jit(solution)/shard_map/mul | solution.py:169
  16.8 1.1 reshape.237
  18.2 1.1 reshape.235
  21.1 0.9 slice.118
  22.7 1.0 copy-done
  23.9 0.8 copy.109
  26.4 1.6 %collective-permute-start.2 = (bf16[18,1,128]{2,1,0:T(2,128)(2,1)}, bf16[18,1,128]{2,1,0:T(2,128)(2,1)}, u32[]{:S(2)}, u32[]{:S(2)}) collective-permute-start(bf16[18,1,128]{2,1,0:T(2,128)(2,1)} %get-tuple-element.15), channel_id=1, source_target_pairs={{1,0},{2,1},{3,2},{0,3},{5,4},{6,5},{7,6},{4,7},{9,8},{10,9},{11,1... | collective-permute-start | bytes 13832 | tf_op jit(solution)/shard_map/ppermute | solution.py:21
  28.0 1.5 %convolution_convert_fusion.1 = bf16[12,32768]{1,0:T(8,128)(2,1)} fusion(bf16[1,4,256,128]{3,2,1,0:T(8,128)(2,1)S(1)} %bitcast.171, s32[12]{0:T(128)S(1)} %sub.52), kind=kOutput, calls=%fused_computation.1 | convolution fusion | flops 3538992 | bytes 1048624 | tf_op jit(solution)/shard_map/dot_general | solution.py:126
  29.5 4.5 %reshape_reshape.6 = bf16[12,2,128,4,32]{4,3,2,1,0:T(4,128)(2,1)S(1)} reshape(bf16[12,32768]{1,0:T(8,128)(2,1)} %convolution_convert_fusion.1) | data formatting | bytes 1572864 | tf_op jit(solution)/shard_map/reshape;reshape | solution.py:35
  34.0 2.9 %copy.97 = bf16[12,2,128,4,32]{2,4,3,0,1:T(8,128)(2,1)} copy(bf16[12,2,128,4,32]{4,3,2,1,0:T(4,128)(2,1)S(1)} %reshape_reshape.6) | data formatting | bytes 1572864 | tf_op jit(solution)/shard_map/reshape;reshape | solution.py:35
  36.9 2.0 %fusion.29 = (f32[128]{0:T(128)}, f32[128]{0:T(128)}, f32[128]{0:T(128)}, f32[128]{0:T(128)}, f32[128]{0:T(128)}, /*index=5*/f32[16,32,128]{2,1,0:T(8,128)S(1)}) fusion(bf16[16,32,128]{2,1,0:T(8,128)(2,1)} %param.10, bf16[18,32,128]{2,1,0:T(8,128)(2,1)} %copy-done.8, bf16[18,1,128]{2,1,0:T(2,128)(2,1)} %collective-permute-done.3, ...), kind=kLoop, calls=%fused_computation.56 | loop fusion | flops 1965440 | bytes 830976 | tf_op jit(solution)/shard_map/reduce_sum | solution.py:173
  41.7 3.3 %all-to-all-start.2 = ((bf16[4,3,2,4,128]{4,3,2,1,0:T(4,128)(2,1)}), bf16[4,3,2,4,128]{4,3,2,1,0:T(4,128)(2,1)S(1)}, u32[]{:S(2)}, u32[]{:S(2)}) async-start(bf16[4,3,2,4,128]{4,3,2,1,0:T(4,128)(2,1)} %reshape.219), calls=%async_computation.2 | async-start | bytes 49152 | tf_op jit(solution)/shard_map/all_to_all | solution.py:120
  45.5 3.3 %all-to-all-done.2 = bf16[4,3,2,4,128]{4,3,2,1,0:T(4,128)(2,1)S(1)} async-done(((bf16[4,3,2,4,128]{4,3,2,1,0:T(4,128)(2,1)}), bf16[4,3,2,4,128]{4,3,2,1,0:T(4,128)(2,1)S(1)}, u32[]{:S(2)}, u32[]{:S(2)}) %all-to-all-start.2) | async-done | bytes 24608 | tf_op jit(solution)/shard_map/all_to_all | solution.py:120
  48.8 3.5 %all-to-all-start.1 = ((bf16[4,3,2,128,128]{4,3,2,1,0:T(8,128)(2,1)}), bf16[4,3,2,128,128]{4,3,2,1,0:T(8,128)(2,1)S(1)}, u32[]{:S(2)}, u32[]{:S(2)}) async-start(bf16[4,3,2,128,128]{4,3,2,1,0:T(8,128)(2,1)} %bitcast.87), calls=%async_computation.1 | async-start | bytes 1572864 | tf_op jit(solution)/shard_map/all_to_all | solution.py:119
  52.6 0.8 copy.105
  53.5 45.1 %psum.7 = f32[5,128]{1,0:T(8,128)S(1)} all-reduce(f32[5,128]{1,0:T(8,128)S(1)} %stack.71), channel_id=1, replica_groups=mesh['gx'=8,'gy'=4] {'gx','gy'}, use_global_device_ids=true, to_apply=%region_7.8 | all-reduce | flops 640 | bytes 5120 | tf_op jit(solution)/shard_map/psum | solution.py:175
  100.2 1.4 %fusion.5 = f32[12,4,32,128]{3,2,1,0:T(8,128)S(1)} fusion(f32[12,4,128,128]{3,2,1,0:T(8,128)S(1)} %fusion.18, f32[12,4,128]{2,1,0:T(4,128)S(1)} %get-tuple-element.19, bf16[12,2,4,32,128]{4,3,2,0,1:T(8,128)(2,1)S(1)} %bitcast.155), kind=kOutput, calls=%fused_computation.9 | convolution fusion | flops 52690944 | bytes 4349952 | tf_op jit(solution)/shard_map/shqk,shdq->shdk/dot_general | solution.py:55
  101.6 2.6 %multiply_convert_fusion = bf16[12,4,128,128]{3,2,1,0:T(8,128)(2,1)S(1)} fusion(f32[12,4,128,128]{3,2,1,0:T(8,128)S(1)} %fusion.18, f32[12,4,128]{2,1,0:T(4,128)S(1)} %get-tuple-element.20, f32[12,4,128]{2,1,0:T(4,128)S(1)} %get-tuple-element.19, bf16[12,2,4,32,128]{4,3,2,0,1:T(8,128)(2,1)S(1)} %bitcast.159, bf16[12,2,4,32,128]{4,3,2,0,1:T(8,128)(2,1)S(1)} %bitcast.156), kind=kOutput, calls=%fused_computation.2 | convolution fusion | flops 54263808 | bytes 5554176 | tf_op jit(solution)/shard_map/shdq,shdk->shqk/dot_general | solution.py:49
  104.2 1.4 %convolution_multiply_fusion.1 = f32[12,4,32,128]{3,2,1,0:T(8,128)} fusion(bf16[12,4,128,128]{3,2,1,0:T(8,128)(2,1)S(1)} %multiply_convert_fusion, bf16[12,2,4,32,128]{4,3,2,0,1:T(8,128)(2,1)S(1)} %bitcast.157), kind=kOutput, calls=%fused_computation.18 | convolution fusion | flops 50528256 | bytes 2752512 | tf_op jit(solution)/shard_map/shqk,shdq->shdk/dot_general | solution.py:59
  105.6 0.9 convolution_multiply_fusion.2
  106.5 1.2 copy.102
  107.7 3.5 %all-to-all-start.3 = ((f32[4,3,128,128]{3,2,1,0:T(8,128)}), f32[4,3,128,128]{3,2,1,0:T(8,128)S(1)}, u32[]{:S(2)}, u32[]{:S(2)}) async-start(f32[4,3,128,128]{3,2,1,0:T(8,128)} %bitcast.37), calls=%async_computation.3 | async-start | bytes 1572864 | tf_op jit(solution)/shard_map/all_to_all | solution.py:140
  111.8 1.6 %copy.106 = f32[12,128,128]{1,0,2:T(8,128)S(1)} copy(f32[12,128,128]{2,1,0:T(8,128)} %bitcast.167) | data formatting | bytes 1572864 | tf_op jit(solution)/shard_map/reshape | solution.py:68
  113.5 1.6 %fusion.1 = f32[4,2,128,128]{3,0,2,1:T(4,128)S(1)} fusion(f32[12,1,128,128]{3,0,2,1:T(8,128)S(1)} %bitcast.162, f32[12,1,128,128]{3,0,2,1:T(8,128)S(1)} %bitcast.163, s32[12]{0:T(128)} %copy-done.16), kind=kOutput, calls=%fused_computation.5 | convolution fusion | flops 19267632 | bytes 2097200 | tf_op jit(solution)/shard_map/sr,sxbf->rxbf/dot_general | solution.py:152
  115.0 1.1 fusion.34
  116.9 1.6 %fusion.24 = bf16[16,32,128]{2,1,0:T(8,128)(2,1)} fusion(f32[16,32,128]{2,1,0:T(8,128)S(1)} %bitcast.175, bf16[16,32,128]{2,1,0:T(8,128)(2,1)S(1)} %copy-done.3, bf16[1,32,128]{2,1,0:T(8,128)(2,1)S(1)} %collective-permute-done.1, bf16[1,32,128]{2,1,0:T(8,128)(2,1)S(1)} %collective-permute-done, f32[128]{0:T(128)S(1)} %copy-done.20, f32[128]{0:T(128)S(1)} %copy-done.21, ...), kind=kLoop, calls=%fused_computation.51 | loop fusion | flops 1835008 | bytes 699904 | tf_op jit(solution)/shard_map/convert_element_type | solution.py:180
  118.4 4.5 %all-to-all-done.3 = f32[4,3,128,128]{3,2,1,0:T(8,128)S(1)} async-done(((f32[4,3,128,128]{3,2,1,0:T(8,128)}), f32[4,3,128,128]{3,2,1,0:T(8,128)S(1)}, u32[]{:S(2)}, u32[]{:S(2)}) %all-to-all-start.3) | async-done | bytes 786464 | tf_op jit(solution)/shard_map/all_to_all | solution.py:140
  122.9 1.8 %fusion.13 = bf16[4,128,128]{2,0,1:T(4,128)(2,1)S(1)} fusion(f32[12,128,128]{2,1,0:T(8,128)S(1)} %bitcast.161, f32[4,128,128]{1,0,2:T(4,128)S(1)} %copy.92, f32[12,4]{0,1:T(4,128)} %copy-done.14), kind=kOutput, calls=%fused_computation.23 | convolution fusion | flops 9568256 | bytes 1179840 | tf_op jit(solution)/shard_map/sr,sbf->rbf/dot_general | solution.py:142
  (112 shorter events, 14.9 us)
Async XLA Ops:
  0.6 19.7 %copy-start.3 = (bf16[16,32,128]{2,1,0:T(8,128)(2,1)S(1)}, bf16[16,32,128]{2,1,0:T(8,128)(2,1)}, u32[]{:S(2)}) copy-start(bf16[16,32,128]{2,1,0:T(8,128)(2,1)} %param.12) | copy-start | bytes 393220
  0.6 19.7 %copy-start.10 = (bf16[16,32,128]{2,1,0:T(8,128)(2,1)S(1)}, bf16[16,32,128]{2,1,0:T(8,128)(2,1)}, u32[]{:S(2)}) copy-start(bf16[16,32,128]{2,1,0:T(8,128)(2,1)} %param.8) | copy-start | bytes 393220
  0.7 18.9 %copy-start.6 = (bf16[16,32,128]{2,1,0:T(8,128)(2,1)S(1)}, bf16[16,32,128]{2,1,0:T(8,128)(2,1)}, u32[]{:S(2)}) copy-start(bf16[16,32,128]{2,1,0:T(8,128)(2,1)} %param.10) | copy-start | bytes 393220
  2.6 22.2 %all-to-all-start = ((bf16[4,1,3]{2,1,0:T(2,128)(2,1)}), bf16[4,1,3]{2,1,0:T(2,128)(2,1)S(1)}, u32[]{:S(2)}, u32[]{:S(2)}) async-start(bf16[4,1,3]{2,1,0:T(2,128)(2,1)} %all_to_all.20), calls=%async_computation | async-start | bytes 4096 | tf_op jit(solution)/shard_map/all_to_all | solution.py:121
  7.6 17.4 %collective-permute-start = (bf16[1,32,128]{2,1,0:T(8,128)(2,1)S(1)}, bf16[1,32,128]{2,1,0:T(8,128)(2,1)S(1)}, u32[]{:S(2)}, u32[]{:S(2)}) collective-permute-start(bf16[1,32,128]{2,1,0:T(8,128)(2,1)S(1)} %get-tuple-element.17), channel_id=1, source_target_pairs={{4,0},{8,4},{12,8},{16,12},{20,16},{24,20},{28,24},{0,28},{5,1},{9... | collective-permute-start | bytes 24584 | tf_op jit(solution)/shard_map/ppermute | solution.py:21
  12.5 12.4 %collective-permute-start.1 = (bf16[1,32,128]{2,1,0:T(8,128)(2,1)S(1)}, bf16[1,32,128]{2,1,0:T(8,128)(2,1)S(1)}, u32[]{:S(2)}, u32[]{:S(2)}) collective-permute-start(bf16[1,32,128]{2,1,0:T(8,128)(2,1)S(1)} %get-tuple-element.18), channel_id=1, source_target_pairs={{0,4},{4,8},{8,12},{12,16},{16,20},{20,24},{24,28},{28,0},{1,5},{5... | collective-permute-start | bytes 24584 | tf_op jit(solution)/shard_map/ppermute | solution.py:18
  13.9 7.0 %copy-start.14 = (f32[12,4]{0,1:T(4,128)}, f32[12,4]{0,1:T(4,128)S(1)}, u32[]{:S(2)}) copy-start(f32[12,4]{0,1:T(4,128)S(1)} %fusion.39) | copy-start | bytes 580
  21.1 3.6 %copy-start.11 = (bf16[16,32,128]{2,1,0:T(8,128)(2,1)S(1)}, bf16[16,32,128]{2,1,0:T(8,128)(2,1)}, u32[]{:S(2)}) copy-start(bf16[16,32,128]{2,1,0:T(8,128)(2,1)} %param.9) | copy-start | bytes 393220
  22.1 1.8 %copy-start.4 = (bf16[4,2,4,32,128]{4,3,2,0,1:T(8,128)(2,1)}, bf16[4,2,4,32,128]{4,3,2,0,1:T(8,128)(2,1)S(1)}, u32[]{:S(2)}) copy-start(bf16[4,2,4,32,128]{4,3,2,0,1:T(8,128)(2,1)S(1)} %get-tuple-element.28) | copy-start | bytes 786436
  24.9 3.1 %copy-start.16 = (s32[12]{0:T(128)}, s32[12]{0:T(128)S(1)}, u32[]{:S(2)}) copy-start(s32[12]{0:T(128)S(1)} %sub.52) | copy-start | bytes 148
  26.2 10.7 %collective-permute-start.3 = (bf16[18,1,128]{2,1,0:T(2,128)(2,1)}, bf16[18,1,128]{2,1,0:T(2,128)(2,1)}, u32[]{:S(2)}, u32[]{:S(2)}) collective-permute-start(bf16[18,1,128]{2,1,0:T(2,128)(2,1)} %get-tuple-element.14), channel_id=1, source_target_pairs={{0,1},{1,2},{2,3},{3,0},{4,5},{5,6},{6,7},{7,4},{8,9},{9,10},{10,1... | collective-permute-start | bytes 13832 | tf_op jit(solution)/shard_map/ppermute | solution.py:18
  26.4 10.5 %collective-permute-start.2 = (bf16[18,1,128]{2,1,0:T(2,128)(2,1)}, bf16[18,1,128]{2,1,0:T(2,128)(2,1)}, u32[]{:S(2)}, u32[]{:S(2)}) collective-permute-start(bf16[18,1,128]{2,1,0:T(2,128)(2,1)} %get-tuple-element.15), channel_id=1, source_target_pairs={{1,0},{2,1},{3,2},{0,3},{5,4},{6,5},{7,6},{4,7},{9,8},{10,9},{11,1... | collective-permute-start | bytes 13832 | tf_op jit(solution)/shard_map/ppermute | solution.py:21
  36.9 3.3 %copy-start.1 = (f32[4,4,128,128]{3,2,1,0:T(8,128)S(1)}, f32[4,4,128,128]{3,2,1,0:T(8,128)}, u32[]{:S(2)}) copy-start(f32[4,4,128,128]{3,2,1,0:T(8,128)} %copy-done) | copy-start | bytes 3145732
  36.9 3.3 %copy-start.5 = (bf16[4,2,4,32,128]{4,3,2,0,1:T(8,128)(2,1)S(1)}, bf16[4,2,4,32,128]{4,3,2,0,1:T(8,128)(2,1)}, u32[]{:S(2)}) copy-start(bf16[4,2,4,32,128]{4,3,2,0,1:T(8,128)(2,1)} %copy-done.4) | copy-start | bytes 786436
  36.9 3.9 %copy-start.13 = (bf16[4,4,128]{2,1,0:T(4,128)(2,1)S(1)}, bf16[4,4,128]{2,1,0:T(4,128)(2,1)}, u32[]{:S(2)}) copy-start(bf16[4,4,128]{2,1,0:T(4,128)(2,1)} %copy-done.12) | copy-start | bytes 12292
  36.9 4.0 %copy-start.15 = (f32[12,4]{0,1:T(4,128)S(1)}, f32[12,4]{0,1:T(4,128)}, u32[]{:S(2)}) copy-start(f32[12,4]{0,1:T(4,128)} %copy-done.14) | copy-start | bytes 580
  40.8 12.7 %copy-start.22 = (f32[128]{0:T(128)S(1)}, f32[128]{0:T(128)}, u32[]{:S(2)}) copy-start(f32[128]{0:T(128)} %get-tuple-element.4) | copy-start | bytes 1540
  40.8 12.7 %copy-start.23 = (f32[128]{0:T(128)S(1)}, f32[128]{0:T(128)}, u32[]{:S(2)}) copy-start(f32[128]{0:T(128)} %get-tuple-element.5) | copy-start | bytes 1540
  40.8 12.6 %copy-start.24 = (f32[128]{0:T(128)S(1)}, f32[128]{0:T(128)}, u32[]{:S(2)}) copy-start(f32[128]{0:T(128)} %get-tuple-element.9) | copy-start | bytes 1540
  40.8 12.6 %copy-start.25 = (f32[128]{0:T(128)S(1)}, f32[128]{0:T(128)}, u32[]{:S(2)}) copy-start(f32[128]{0:T(128)} %get-tuple-element.10) | copy-start | bytes 1540
  40.8 12.6 %copy-start.26 = (f32[128]{0:T(128)S(1)}, f32[128]{0:T(128)}, u32[]{:S(2)}) copy-start(f32[128]{0:T(128)} %get-tuple-element.11) | copy-start | bytes 1540
  41.0 58.6 %copy-start.2 = (bf16[12,2,128,4,32]{2,4,3,0,1:T(8,128)(2,1)S(1)}, bf16[12,2,128,4,32]{2,4,3,0,1:T(8,128)(2,1)}, u32[]{:S(2)}) copy-start(bf16[12,2,128,4,32]{2,4,3,0,1:T(8,128)(2,1)} %copy.97) | copy-start | bytes 2359300
  41.7 7.2 %all-to-all-start.2 = ((bf16[4,3,2,4,128]{4,3,2,1,0:T(4,128)(2,1)}), bf16[4,3,2,4,128]{4,3,2,1,0:T(4,128)(2,1)S(1)}, u32[]{:S(2)}, u32[]{:S(2)}) async-start(bf16[4,3,2,4,128]{4,3,2,1,0:T(4,128)(2,1)} %reshape.219), calls=%async_computation.2 | async-start | bytes 49152 | tf_op jit(solution)/shard_map/all_to_all | solution.py:120
  48.8 50.4 %all-to-all-start.1 = ((bf16[4,3,2,128,128]{4,3,2,1,0:T(8,128)(2,1)}), bf16[4,3,2,128,128]{4,3,2,1,0:T(8,128)(2,1)S(1)}, u32[]{:S(2)}, u32[]{:S(2)}) async-start(bf16[4,3,2,128,128]{4,3,2,1,0:T(8,128)(2,1)} %bitcast.87), calls=%async_computation.1 | async-start | bytes 1572864 | tf_op jit(solution)/shard_map/all_to_all | solution.py:119
  107.7 15.2 %all-to-all-start.3 = ((f32[4,3,128,128]{3,2,1,0:T(8,128)}), f32[4,3,128,128]{3,2,1,0:T(8,128)S(1)}, u32[]{:S(2)}, u32[]{:S(2)}) async-start(f32[4,3,128,128]{3,2,1,0:T(8,128)} %bitcast.37), calls=%async_computation.3 | async-start | bytes 1572864 | tf_op jit(solution)/shard_map/all_to_all | solution.py:140
  111.2 3.8 %copy-start.7 = (f32[4,128,128]{1,0,2:T(4,128)S(1)}, f32[4,128,128]{1,0,2:T(4,128)}, u32[]{:S(2)}) copy-start(f32[4,128,128]{1,0,2:T(4,128)} %copy.109) | copy-start | bytes 786436
  113.4 3.4 %copy-start.9 = (bf16[18,32,128]{2,1,0:T(8,128)(2,1)S(1)}, bf16[18,32,128]{2,1,0:T(8,128)(2,1)}, u32[]{:S(2)}) copy-start(bf16[18,32,128]{2,1,0:T(8,128)(2,1)} %copy-done.8) | copy-start | bytes 442372
  113.4 3.4 %copy-start.17 = (f32[128]{0:T(128)S(1)}, f32[128]{0:T(128)}, u32[]{:S(2)}) copy-start(f32[128]{0:T(128)} %get-tuple-element.21) | copy-start | bytes 1540
  113.4 3.4 %copy-start.18 = (f32[128]{0:T(128)S(1)}, f32[128]{0:T(128)}, u32[]{:S(2)}) copy-start(f32[128]{0:T(128)} %get-tuple-element.22) | copy-start | bytes 1540
  113.4 3.4 %copy-start.19 = (f32[128]{0:T(128)S(1)}, f32[128]{0:T(128)}, u32[]{:S(2)}) copy-start(f32[128]{0:T(128)} %get-tuple-element.23) | copy-start | bytes 1540
  113.4 3.4 %copy-start.20 = (f32[128]{0:T(128)S(1)}, f32[128]{0:T(128)}, u32[]{:S(2)}) copy-start(f32[128]{0:T(128)} %get-tuple-element.24) | copy-start | bytes 1540
  113.4 3.4 %copy-start.21 = (f32[128]{0:T(128)S(1)}, f32[128]{0:T(128)}, u32[]{:S(2)}) copy-start(f32[128]{0:T(128)} %get-tuple-element.25) | copy-start | bytes 1540
  (3 other events, 2.2 us)
where the time goes:
time: 126 us; the launch traced here: 125 us
  blocking collectives  45.1 us (36%)
  local copies, waits for them, and re-layouts  28.9 us (23%)
  starting transfers between devices  21.2 us (17%)
  matrix products  14.7 us (12%)
  waiting for transfers between devices  7.84 us (6%)
  other arithmetic  6.33 us (5%)
    psum x1, blocking collectives, per_device(): summed = lax.psum(partial_rows, ('gx', 'gy'))  45.1 us
    another operation x2, local copies, waits for them, and re-layouts, tile_grads(): key_pack.reshape(item_count, 2, block_rows, HEADS, head_width)  7.41 us
    ppermute x2, starting transfers between devices, with_halo(): lax.ppermute(lax.slice_in_dim(block, 0, width, axis=dim), axis, backward)  6.53 us
    all_to_all x1, waiting for transfers between devices, per_device(): lax.all_to_all(query_part, 'gy', split_axis=0, concat_axis=0, tiled=True)  4.48 us
    unnamed x60, local copies, waits for them, and re-layouts  4.41 us
    all_to_all x1, starting transfers between devices, per_device(): lax.all_to_all(send_ids, 'gy', split_axis=0, concat_axis=0, tiled=True)  4.24 us
    reshape x5, local copies, waits for them, and re-layouts, points_last(): return part.reshape(item_count, features, block_rows).transpose(0, 2, 1)  3.97 us
    all_to_all x1, starting transfers between devices, per_device(): lax.all_to_all(query_part, 'gy', split_axis=0, concat_axis=0, tiled=True)  3.54 us
  transfers between devices with their start and end apart: 8, of which 2 were waited for; matrix products, arithmetic and copies ran while one was open for 24% of the time, Pallas kernels for 0%

commit v1 on v0

v1 whole, which is shorter than its diff:
```python
import functools
import math

import jax
import jax.numpy as jnp
from jax import lax
from jax.experimental import pallas as pl
from jax.experimental.pallas import tpu as pltpu
from jax.sharding import PartitionSpec as P

BLOCK = 128
HEADS = 4
LOG2E = 1.4426950408889634
F32 = jnp.float32
BF16 = jnp.bfloat16


def dot(a, b):
    return jnp.dot(a, b, preferred_element_type=F32)


def dot_nt(a, b):
    return lax.dot_general(a, b, (((1,), (1,)), ((), ())), preferred_element_type=F32)


def iota(shape, dim):
    return lax.broadcasted_iota(jnp.int32, shape, dim)


def kernel(
    nx, n, tx, ty, rb, listed, cap,
    q_ref, k_ref, v_ref, o_ref, g_ref, ln_ref, nb_ref, w_ref,
    dq_ref, dk_ref, dv_ref, sg_ref,
    q_in, g_in, st_own, st_all, nb_all, nb_own, nb_s, kmt, edge, xh, yh,
    dq_acc, dk_acc, dv_acc, dk_part, dv_part, ret_out, ret_in,
    part, col_all, row_sum, row_all,
    big_send, big_recv, small_send, small_recv, halo_send, halo_recv,
    ret_send, ret_recv, col_send, col_recv, row_send, row_recv, local_sem,
):
    f = q_ref.shape[2]
    pts = rb * BLOCK
    hw = f // HEADS
    scale = 1.0 / math.sqrt(hw)
    mx = lax.axis_index("gx")
    my = lax.axis_index("gy")
    half = n // 2
    sib = my + 1 - 2 * lax.rem(my, 2)

    def peer(t):
        return lax.rem(my + t, n)

    def xpeer(t):
        return lax.rem(mx + t, nx)

    barrier = pltpu.get_barrier_semaphore()
    for t in range(1, n):
        pl.semaphore_signal(barrier, inc=1, device_id=(mx, peer(t)), device_id_type=pl.DeviceIdType.MESH)

    def greet(t, carry):
        pl.semaphore_signal(barrier, inc=1, device_id=(xpeer(t), my), device_id_type=pl.DeviceIdType.MESH)
        return carry

    lax.fori_loop(1, nx, greet, 0)

    def remote(src, dst, ssem, rsem, x, y):
        return pltpu.make_async_remote_copy(
            src_ref=src, dst_ref=dst, send_sem=ssem, recv_sem=rsem,
            device_id=(x, y), device_id_type=pl.DeviceIdType.MESH,
        )

    nb_own[...] = jnp.zeros_like(nb_own)
    nb_own[0:rb, 0:listed] = nb_ref[0]
    g2 = g_ref[...].reshape(pts, f)
    rows_of = iota((2 * tx, pts), 0)
    want = jnp.where(rows_of < tx, rows_of * ty, (rows_of - tx) * ty + ty - 1)
    pick = (iota((2 * tx, pts), 1) == want).astype(F32).astype(BF16)
    edge[...] = dot(pick, g2).astype(BF16).reshape(2, tx, f)

    prod = g2.astype(F32) * o_ref[...].reshape(pts, f).astype(F32)
    high = prod.astype(BF16)
    low = (prod - high.astype(F32)).astype(BF16)
    head_row = iota((2 * HEADS, f), 0) - HEADS
    summing = (iota((2 * HEADS, f), 1) // hw == head_row).astype(F32).astype(BF16)
    lines = BLOCK // ty
    ln = ln_ref[...].astype(F32).reshape(HEADS * tx, ty)
    ln = jnp.concatenate([ln] * lines, axis=1)
    ln = jnp.where(
        iota(ln.shape, 1) // ty == lax.rem(iota(ln.shape, 0), lines), ln, 0.0
    ).astype(BF16)
    gr = iota((rb * 2 * HEADS, HEADS * tx), 0)
    gc = iota((rb * 2 * HEADS, HEADS * tx), 1)
    gather = (
        (gc // tx == lax.rem(gr, 2 * HEADS)) & (lax.rem(gc, tx) // lines == gr // (2 * HEADS))
    ).astype(F32).astype(BF16)
    ln_rows = dot(gather, ln) * LOG2E
    for b in range(rb):
        sl = slice(b * BLOCK, (b + 1) * BLOCK)
        delta = dot_nt(summing, high[sl]) + dot_nt(summing, low[sl])
        delta = delta.astype(BF16).astype(F32)
        st_own[b] = ln_rows[b * 2 * HEADS:(b + 1) * 2 * HEADS] + delta

    pl.semaphore_wait(barrier, n - 1 + nx - 1)

    big = []
    targets = [(0, sib)] + [(t, peer(2 * t)) for t in range(1, half)]
    for t, to in targets[1:] + targets[:1]:
        at = 1 + t
        big.append(remote(q_ref, q_in[t], big_send.at[at, 0], big_recv.at[at, 0], mx, to))
        big.append(remote(g_ref, g_in[t], big_send.at[at, 1], big_recv.at[at, 1], mx, to))
    halo = [
        remote(edge.at[0], yh.at[0], halo_send.at[0], halo_recv.at[0], mx, peer(n - 1)),
        remote(edge.at[1], yh.at[1], halo_send.at[1], halo_recv.at[1], mx, peer(1)),
        remote(g_ref.at[0, pl.ds(0, ty)], xh.at[0], halo_send.at[2], halo_recv.at[2], xpeer(nx - 1), my),
        remote(g_ref.at[rb - 1, pl.ds(BLOCK - ty, ty)], xh.at[1], halo_send.at[3], halo_recv.at[3], xpeer(1), my),
    ]
    small = []
    for t in range(1, n):
        small.append(remote(nb_own, nb_all.at[my], small_send.at[t, 0], small_recv.at[t, 0], mx, peer(t)))
        small.append(remote(st_own, st_all.at[my], small_send.at[t, 1], small_recv.at[t, 1], mx, peer(t)))
    for copy in halo + small + big:
        copy.start()

    def wait_big(number, which):
        ref = (q_in, g_in)[which][number - 1]
        remote(
            ref, ref, big_send.at[number, which], big_recv.at[number, which], mx, sib
        ).wait_recv()

    lane_head = iota((BLOCK, f), 1) // hw
    row_head = iota((f, BLOCK), 0) // hw

    def by_head(x):
        return [jnp.where(lane_head == h, x, jnp.zeros_like(x)) for h in range(HEADS)]

    def item(q, g, st, k, v, kt):
        qs, gs = by_head(q), by_head(g)
        probs, grads = [], []
        for h in range(HEADS):
            s = dot_nt(k, qs[h])
            dp = dot_nt(v, gs[h])
            p = jnp.exp2(s * (scale * LOG2E) - st[h:h + 1])
            d = p * (dp - st[HEADS + h:HEADS + h + 1])
            probs.append(p.astype(BF16))
            grads.append(d.astype(BF16))
        dv = dot(jnp.concatenate(probs, 1), jnp.concatenate(gs, 0))
        dk = dot(jnp.concatenate(grads, 1), jnp.concatenate(qs, 0)) * scale
        dqt = dot(kt, jnp.concatenate(grads, 0)) * scale
        return dqt, dk, dv

    for b in range(rb):
        k = k_ref[b]
        ktr = k.astype(F32).T.astype(BF16)
        kt = jnp.concatenate(
            [jnp.where(row_head == h, ktr, jnp.zeros_like(ktr)) for h in range(HEADS)], 1
        )
        kmt[b] = kt
        dqt, dk, dv = item(q_ref[b], g_ref[b], st_own[b], k, v_ref[b], kt)
        dq_acc[b] = dqt
        dk_acc[b] = dk
        dv_acc[b] = dv

    for copy in halo:
        copy.wait_recv()
    g32 = g2.astype(F32)
    v32 = v_ref[...].reshape(pts, f).astype(F32)
    pr = iota((pts, tx), 0)
    pc = iota((pts, tx), 1)
    put_next = (pr == pc * ty + ty - 1).astype(F32).astype(BF16)
    put_prev = (pr == pc * ty).astype(F32).astype(BF16)
    ycol = lax.rem(iota((pts, f), 0), ty)
    y_next = jnp.where(ycol == ty - 1, dot(put_next, yh[0]), pltpu.roll(g32, pts - 1, 0))
    y_prev = jnp.where(ycol == 0, dot(put_prev, yh[1]), pltpu.roll(g32, 1, 0))
    x_next = jnp.concatenate([g32[ty:], xh[0].astype(F32)], 0)
    x_prev = jnp.concatenate([xh[1].astype(F32), g32[:-ty]], 0)
    part[...] = jnp.zeros_like(part)
    term = None
    for index, moved in enumerate([g32, x_next, x_prev, y_next, y_prev]):
        part[index:index + 1] = jnp.sum(moved * v32, axis=0, keepdims=True)
        scaled = w_ref[index:index + 1] * moved
        term = scaled if term is None else term + scaled
    for b in range(rb):
        dv_acc[b] += term[b * BLOCK:(b + 1) * BLOCK]

    cols = [
        remote(part, col_all.at[my], col_send.at[t], col_recv.at[t], mx, peer(t)) for t in range(1, n)
    ]
    for copy in cols:
        copy.start()
    col_all[my] = part[...]

    for t in range(1, n):
        small[2 * (t - 1)].wait_recv()
    nb_all[my] = nb_own[...]
    to_smem = pltpu.make_async_copy(nb_all, nb_s, local_sem)
    to_smem.start()
    to_smem.wait()

    def slots(src):
        rows = [jnp.int32(0)] * cap
        inner = [jnp.int32(0)] * cap
        count = jnp.int32(0)
        for r in range(rb):
            for j in range(listed):
                value = nb_s[src, r, j]
                mine = lax.div(value, rb) == my
                for c in range(cap):
                    here = mine & (count == c)
                    rows[c] = jnp.where(here, r, rows[c])
                    inner[c] = jnp.where(here, lax.rem(value, rb), inner[c])
                count = count + mine.astype(jnp.int32)
        return rows, inner, count

    forwards = []

    def pass_on(which):
        for t in range(1, half):
            wait_big(1 + t, which)
            ref = (q_in, g_in)[which]
            copy = remote(
                ref[t], ref[half + t - 1],
                big_send.at[half + t, which], big_recv.at[half + t, which], mx, sib,
            )
            copy.start()
            forwards.append(copy)

    keyed = []
    returns = []

    def work(src, number):
        rows, inner, count = slots(src)
        own = number == 0
        q_from = q_ref if own else q_in[number - 1]
        g_from = g_ref if own else g_in[number - 1]
        for c in range(cap):
            at = number * cap + c
            r, i = rows[c], inner[c]
            q, g = q_from[r], g_from[r]
            st = st_own[r] if own else st_all[src, r]
            dqt, dk, dv = item(q, g, st, k_ref[i], v_ref[i], kmt[i])
            dk_part[at] = dk
            dv_part[at] = dv
            keyed.append(jnp.where(count > c, i, -1))
            if own:
                ret_in[my * cap + c] = dqt.astype(BF16)
            else:
                ret_out[at] = dqt.astype(BF16)
                copy = remote(
                    ret_out.at[at], ret_in.at[my * cap + c],
                    ret_send.at[at], ret_recv.at[at], mx, src,
                )
                copy.start()
                returns.append(copy)

    work(my, 0)
    pass_on(0)
    wait_big(1, 0)
    wait_big(1, 1)
    for t in range(1, n):
        small[2 * (t - 1) + 1].wait_recv()
    work(sib, 1)
    pass_on(1)

    for copy in cols:
        copy.wait_recv()
    total = col_all[0]
    for d in range(1, n):
        total = total + col_all[d]
    row_sum[...] = total
    row_all[mx] = total

    def row_copy(t):
        return remote(row_sum, row_all.at[mx], row_send.at[t], row_recv.at[t], xpeer(t), my)

    def send_row(t, carry):
        row_copy(t).start()
        return carry

    lax.fori_loop(1, nx, send_row, 0)

    for t in range(1, half):
        work(lax.rem(my + n - 2 * t, n), 1 + t)
    for t in range(1, half):
        wait_big(half + t, 0)
        wait_big(half + t, 1)
        work(lax.rem(sib + n - 2 * t, n), half + t)

    for b in range(rb):
        dk = dk_acc[b]
        dv = dv_acc[b]
        for at in range(n * cap):
            hit = jnp.full((BLOCK, f), keyed[at], jnp.int32) == b
            dk = dk + jnp.where(hit, dk_part[at], 0.0)
            dv = dv + jnp.where(hit, dv_part[at], 0.0)
        dk_ref[b * BLOCK:(b + 1) * BLOCK] = dk.astype(BF16)
        dv_ref[b * BLOCK:(b + 1) * BLOCK] = dv.astype(BF16)

    def get_row(t, carry):
        row_copy(t).wait_recv()
        return carry

    lax.fori_loop(1, nx, get_row, 0)
    total = lax.fori_loop(1, nx, lambda d, acc: acc + row_all[d], row_all[0])
    sg_ref[...] = total / math.sqrt(pts * nx * n)

    for copy in returns:
        copy.wait_recv()
    place = []
    for r in range(rb):
        for j in range(listed):
            value = nb_s[my, r, j]
            place.append(lax.div(value, rb))
    for r in range(rb):
        dqt = dq_acc[r]
        for j in range(listed):
            e = r * listed + j
            rank = jnp.int32(0)
            for before in range(e):
                rank = rank + (place[before] == place[e]).astype(jnp.int32)
            dqt = dqt + ret_in[place[e] * cap + rank].astype(F32)
        dq_ref[r * BLOCK:(r + 1) * BLOCK] = dqt.T.astype(BF16)

    for copy in halo + small + big + cols + forwards + returns:
        copy.wait_send()

    def end_row(t, carry):
        row_copy(t).wait_send()
        return carry

    lax.fori_loop(1, nx, end_row, 0)


def per_device(nx, n, queries, keys, values, out_attn, out_grad, log_norm, neighbour_blocks, stencil):
    tx, ty, f = queries.shape
    pts = tx * ty
    rb = pts // BLOCK
    listed = neighbour_blocks.shape[2]
    cap = max(2, (rb * listed + n - 1) // n)
    flat = [a.reshape(rb, BLOCK, f) for a in (queries, keys, values, out_attn, out_grad)]
    vmem = pl.BlockSpec(memory_space=pltpu.VMEM)
    half = n // 2
    dma = pltpu.SemaphoreType.DMA
    grads = jax.ShapeDtypeStruct((pts, f), BF16)
    dq, dk, dv, sg = pl.pallas_call(
        functools.partial(kernel, nx, n, tx, ty, rb, listed, cap),
        out_shape=[grads, grads, grads, jax.ShapeDtypeStruct((8, f), F32)],
        in_specs=[vmem] * 8,
        out_specs=[vmem] * 4,
        scratch_shapes=[
            [pltpu.VMEM((rb, BLOCK, f), BF16)] * (n - 1),
            [pltpu.VMEM((rb, BLOCK, f), BF16)] * (n - 1),
            pltpu.VMEM((rb, 2 * HEADS, BLOCK), F32),
            pltpu.VMEM((n, rb, 2 * HEADS, BLOCK), F32),
            pltpu.VMEM((n, 8, 128), jnp.int32),
            pltpu.VMEM((8, 128), jnp.int32),
            pltpu.SMEM((n, 8, 128), jnp.int32),
            pltpu.VMEM((rb, f, HEADS * BLOCK), BF16),
            pltpu.VMEM((2, tx, f), BF16),
            pltpu.VMEM((2, ty, f), BF16),
            pltpu.VMEM((2, tx, f), BF16),
            pltpu.VMEM((rb, f, BLOCK), F32),
            pltpu.VMEM((rb, BLOCK, f), F32),
            pltpu.VMEM((rb, BLOCK, f), F32),
            pltpu.VMEM((n * cap, BLOCK, f), F32),
            pltpu.VMEM((n * cap, BLOCK, f), F32),
            pltpu.VMEM((n * cap, f, BLOCK), BF16),
            pltpu.VMEM((n * cap, f, BLOCK), BF16),
            pltpu.VMEM((8, f), F32),
            pltpu.VMEM((n, 8, f), F32),
            pltpu.VMEM((8, f), F32),
            pltpu.VMEM((nx, 8, f), F32),
            dma((n, 2)), dma((n, 2)),
            dma((n, 2)), dma((n, 2)),
            dma((4,)), dma((4,)),
            dma((n * cap,)), dma((n * cap,)),
            dma((n,)), dma((n,)),
            dma((nx,)), dma((nx,)),
            dma,
        ],
        compiler_params=pltpu.CompilerParams(
            collective_id=0, has_side_effects=True, vmem_limit_bytes=40 * 1024 * 1024
        ),
    )(*flat, log_norm, neighbour_blocks, stencil)
    shape = (tx, ty, f)
    return dq.reshape(shape), dk.reshape(shape), dv.reshape(shape), sg[:5]


def solution(mesh):
    placed = (
        P("gx", "gy", None),
        P("gx", "gy", None),
        P("gx", "gy", None),
        P("gx", "gy", None),
        P("gx", "gy", None),
        P(None, "gx", "gy"),
        P("gx", "gy", None),
        P(),
    )
    return jax.shard_map(
        functools.partial(per_device, mesh.shape["gx"], mesh.shape["gy"]),
        mesh=mesh,
        in_specs=placed,
        out_specs=(P("gx", "gy", None), P("gx", "gy", None), P("gx", "gy", None), P()),
        check_vma=False,
    )
```

time: 126 us -> 31.1 us (0.25)
  blocking collectives: 45.1 us -> 0 us
  Pallas kernels: 0 us -> 21.6 us
  starting transfers between devices: 21.2 us -> 0 us
  local copies, waits for them, and re-layouts: 28.9 us -> 8.56 us
  matrix products: 14.7 us -> 0 us
  waiting for transfers between devices: 7.84 us -> 0 us
  other arithmetic: 6.33 us -> 0 us
    psum x1 -> x0, blocking collectives: 45.1 us -> none  [per_device(): summed = lax.psum(partial_rows, ('gx', 'gy'))]
    pallas_call x0 -> x1, Pallas kernels: none -> 21.6 us  [per_device(): pl.pallas_call(functools.partial(kernel, nx, n, tx, ty, rb, listed, cap),...]
    dot_general x17 -> x0, matrix products: 14.7 us -> none  [the longest x2 3.08 us: tile_grads(): jnp.einsum('shdq,shdk->shqk', grad_heads, value_heads, preferred_element_...]
    all_to_all x4 -> x0, starting transfers between devices: 14.5 us -> none  [the longest x1 4.24 us: per_device(): lax.all_to_all(send_ids, 'gy', split_axis=0, concat_axis=0, tiled=True)]
    another operation x11 -> x0, local copies, waits for them, and re-layouts: 12 us -> none  [the longest x2 7.41 us: tile_grads(): key_pack.reshape(item_count, 2, block_rows, HEADS, head_width)]
    all_to_all x4 -> x0, waiting for transfers between devices: 7.83 us -> none  [the longest x1 4.48 us: per_device(): lax.all_to_all(query_part, 'gy', split_axis=0, concat_axis=0, tiled=True)]
    ppermute x4 -> x0, starting transfers between devices: 6.72 us -> none  [the longest x2 6.53 us: with_halo(): lax.ppermute(lax.slice_in_dim(block, 0, width, axis=dim), axis, backward)]
    reshape x9 -> x0, local copies, waits for them, and re-layouts: 5.92 us -> none  [the longest x5 3.97 us: points_last(): return part.reshape(item_count, features, block_rows).transpose(0, 2, 1)]
  transfers between devices with their start and end apart: 8 -> 0, of which waited for: 2 -> 0; matrix products, arithmetic and copies ran while one was open for 24% -> 0% of each run, Pallas kernels for 0% -> 0%
where the time goes in v1:
time: 31.1 us; the launch traced here: 30.8 us
  Pallas kernels  21.6 us (69%)
  local copies, waits for them, and re-layouts  8.56 us (28%)
  between operations  0.66 us (2%)
    pallas_call x1, Pallas kernels, per_device(): pl.pallas_call(functools.partial(kernel, nx, n, tx, ty, rb, listed, cap),...  21.6 us
    unnamed x21, local copies, waits for them, and re-layouts  8.56 us

profile of v1, /device:TPU:0, one launch (start us, length us, event | category | flops | bytes accessed | tf_op | source)
XLA Modules:
  0.0 30.8 jit_solution(12984682603564678477)
XLA Ops:
  0.6 0.0 copy-start.7
  0.6 0.0 copy-start.6
  0.7 0.7 %copy-done.7 = s32[1,4,3]{1,0,2:T(1,128)S(1)} copy-done((s32[1,4,3]{1,0,2:T(1,128)S(1)}, s32[1,4,3]{1,0,2:T(1,128)}, u32[]{:S(2)}) %copy-start.7) | copy-done | bytes 72
  1.3 0.1 copy.12.nb_ref
  1.4 0.0 copy-done.6
  1.4 0.0 copy-start
  1.4 0.9 %copy-done = bf16[16,32,128]{2,1,0:T(8,128)(2,1)S(1)} copy-done((bf16[16,32,128]{2,1,0:T(8,128)(2,1)S(1)}, bf16[16,32,128]{2,1,0:T(8,128)(2,1)}, u32[]{:S(2)}) %copy-start) | copy-done | bytes 131096
  2.3 0.0 copy-start.1
  2.3 0.9 %copy-done.1 = bf16[16,32,128]{2,1,0:T(8,128)(2,1)S(1)} copy-done((bf16[16,32,128]{2,1,0:T(8,128)(2,1)S(1)}, bf16[16,32,128]{2,1,0:T(8,128)(2,1)}, u32[]{:S(2)}) %copy-start.1) | copy-done | bytes 131096
  3.2 0.0 copy-start.2
  3.2 0.9 %copy-done.2 = bf16[16,32,128]{2,1,0:T(8,128)(2,1)S(1)} copy-done((bf16[16,32,128]{2,1,0:T(8,128)(2,1)S(1)}, bf16[16,32,128]{2,1,0:T(8,128)(2,1)}, u32[]{:S(2)}) %copy-start.2) | copy-done | bytes 131096
  4.1 0.0 copy-start.3
  4.1 0.9 %copy-done.3 = bf16[16,32,128]{2,1,0:T(8,128)(2,1)S(1)} copy-done((bf16[16,32,128]{2,1,0:T(8,128)(2,1)S(1)}, bf16[16,32,128]{2,1,0:T(8,128)(2,1)}, u32[]{:S(2)}) %copy-start.3) | copy-done | bytes 131096
  5.0 0.0 copy-start.4
  5.0 0.9 %copy-done.4 = bf16[16,32,128]{2,1,0:T(8,128)(2,1)S(1)} copy-done((bf16[16,32,128]{2,1,0:T(8,128)(2,1)S(1)}, bf16[16,32,128]{2,1,0:T(8,128)(2,1)}, u32[]{:S(2)}) %copy-start.4) | copy-done | bytes 131096
  5.9 0.0 copy-start.5
  5.9 0.7 %copy-done.5 = bf16[4,16,32]{2,1,0:T(8,128)(2,1)S(1)} copy-done((bf16[4,16,32]{2,1,0:T(8,128)(2,1)S(1)}, bf16[4,16,32]{2,1,0:T(8,128)(2,1)}, u32[]{:S(2)}) %copy-start.5) | copy-done | bytes 4120
  6.7 21.6 %shard_map.111 = (bf16[512,128]{1,0:T(8,128)(2,1)S(1)}, bf16[512,128]{1,0:T(8,128)(2,1)S(1)}, bf16[512,128]{1,0:T(8,128)(2,1)S(1)}, f32[8,128]{1,0:T(8,128)S(1)}) custom-call(bf16[4,128,128]{2,1,0:T(8,128)(2,1)S(1)} %bitcast.12, bf16[4,128,128]{2,1,0:T(8,128)(2,1)S(1)} %bitcast.13, bf16[4,128,128]{2,1,0:T(8,128)(2,1)S(1)} %bitcast.14, ...), custom_call_target="tpu_custom_call" | custom-call | tf_op jit(solution)/shard_map/pallas_call | solution.py:343
  28.3 0.7 %copy.17 = bf16[16,32,128]{2,1,0:T(8,128)(2,1)} copy(bf16[16,32,128]{2,1,0:T(8,128)(2,1)S(1)} %bitcast.11) | data formatting | bytes 262144
  28.9 0.7 %copy.18 = bf16[16,32,128]{2,1,0:T(8,128)(2,1)} copy(bf16[16,32,128]{2,1,0:T(8,128)(2,1)S(1)} %bitcast.10) | data formatting | bytes 262144
  29.6 0.7 %copy.19 = bf16[16,32,128]{2,1,0:T(8,128)(2,1)} copy(bf16[16,32,128]{2,1,0:T(8,128)(2,1)S(1)} %bitcast.9) | data formatting | bytes 262144
  30.2 0.6 %copy.20 = f32[5,128]{1,0:T(8,128)} copy(f32[5,128]{1,0:T(8,128)S(1)} %bitcast.17) | data formatting | bytes 5120
Async XLA Ops:
  0.6 0.7 %copy-start.7 = (s32[1,4,3]{1,0,2:T(1,128)S(1)}, s32[1,4,3]{1,0,2:T(1,128)}, u32[]{:S(2)}) copy-start(s32[1,4,3]{1,0,2:T(1,128)} %param.14) | copy-start | bytes 148
  0.6 0.8 %copy-start.6 = (f32[5,128]{1,0:T(8,128)S(1)}, f32[5,128]{1,0:T(8,128)}, u32[]{:S(2)}) copy-start(f32[5,128]{1,0:T(8,128)} %w_ref.1) | copy-start | bytes 7684
  1.4 0.9 %copy-start = (bf16[16,32,128]{2,1,0:T(8,128)(2,1)S(1)}, bf16[16,32,128]{2,1,0:T(8,128)(2,1)}, u32[]{:S(2)}) copy-start(bf16[16,32,128]{2,1,0:T(8,128)(2,1)} %param.8) | copy-start | bytes 393220
  2.3 0.9 %copy-start.1 = (bf16[16,32,128]{2,1,0:T(8,128)(2,1)S(1)}, bf16[16,32,128]{2,1,0:T(8,128)(2,1)}, u32[]{:S(2)}) copy-start(bf16[16,32,128]{2,1,0:T(8,128)(2,1)} %param.9) | copy-start | bytes 393220
  3.2 0.9 %copy-start.2 = (bf16[16,32,128]{2,1,0:T(8,128)(2,1)S(1)}, bf16[16,32,128]{2,1,0:T(8,128)(2,1)}, u32[]{:S(2)}) copy-start(bf16[16,32,128]{2,1,0:T(8,128)(2,1)} %param.10) | copy-start | bytes 393220
  4.1 0.9 %copy-start.3 = (bf16[16,32,128]{2,1,0:T(8,128)(2,1)S(1)}, bf16[16,32,128]{2,1,0:T(8,128)(2,1)}, u32[]{:S(2)}) copy-start(bf16[16,32,128]{2,1,0:T(8,128)(2,1)} %param.11) | copy-start | bytes 393220
  5.0 0.9 %copy-start.4 = (bf16[16,32,128]{2,1,0:T(8,128)(2,1)S(1)}, bf16[16,32,128]{2,1,0:T(8,128)(2,1)}, u32[]{:S(2)}) copy-start(bf16[16,32,128]{2,1,0:T(8,128)(2,1)} %param.12) | copy-start | bytes 393220
  5.9 0.7 %copy-start.5 = (bf16[4,16,32]{2,1,0:T(8,128)(2,1)S(1)}, bf16[4,16,32]{2,1,0:T(8,128)(2,1)}, u32[]{:S(2)}) copy-start(bf16[4,16,32]{2,1,0:T(8,128)(2,1)} %ln_ref.1) | copy-start | bytes 12292

commit v2 on v1

--- a/solution.py
+++ b/solution.py
@@ -29,14 +29,23 @@
 
 def kernel(
     nx, n, tx, ty, rb, listed, cap,
-    q_ref, k_ref, v_ref, o_ref, g_ref, ln_ref, nb_ref, w_ref,
-    dq_ref, dk_ref, dv_ref, sg_ref,
+    q_hbm, k_hbm, v_hbm, o_hbm, g_hbm, ln_hbm, w_hbm, nb_ref,
+    dq_hbm, dk_hbm, dv_hbm, sg_hbm,
+    dq_ref, dk_ref, dv_ref, sg_ref, store_sem,
+    q_ref, k_ref, v_ref, o_ref, g_ref, ln_ref, w_ref, load_sem,
     q_in, g_in, st_own, st_all, nb_all, nb_own, nb_s, kmt, edge, xh, yh,
     dq_acc, dk_acc, dv_acc, dk_part, dv_part, ret_out, ret_in,
     part, col_all, row_sum, row_all,
     big_send, big_recv, small_send, small_recv, halo_send, halo_recv,
     ret_send, ret_recv, col_send, col_recv, row_send, row_recv, local_sem,
 ):
+    g_load, o_load, ln_load, k_load, v_load, q_load, w_load = [
+        pltpu.make_async_copy(src, dst, load_sem.at[at])
+        for at, (src, dst) in enumerate([
+            (g_hbm, g_ref), (o_hbm, o_ref), (ln_hbm, ln_ref), (k_hbm, k_ref),
+            (v_hbm, v_ref), (q_hbm, q_ref), (w_hbm, w_ref),
+        ])
+    ]
     f = q_ref.shape[2]
     pts = rb * BLOCK
     hw = f // HEADS
@@ -68,8 +77,34 @@
             device_id=(x, y), device_id_type=pl.DeviceIdType.MESH,
         )
 
+    for copy in (g_load, o_load, ln_load, k_load, v_load, q_load, w_load):
+        copy.start()
     nb_own[...] = jnp.zeros_like(nb_own)
     nb_own[0:rb, 0:listed] = nb_ref[0]
+    pl.semaphore_wait(barrier, n - 1 + nx - 1)
+
+    lists = [
+        remote(nb_own, nb_all.at[my], small_send.at[t, 0], small_recv.at[t, 0], mx, peer(t))
+        for t in range(1, n)
+    ]
+    big = []
+
+    def send_big(t, which):
+        to = sib if t == 0 else peer(2 * t)
+        src, dst = ((q_hbm, q_in), (g_hbm, g_in))[which]
+        big.append(remote(
+            src, dst[t], big_send.at[1 + t, which], big_recv.at[1 + t, which], mx, to
+        ))
+        big[-1].start()
+
+    for copy in lists:
+        copy.start()
+    for t in range(1, half):
+        send_big(t, 0)
+
+    g_load.wait()
+    o_load.wait()
+    ln_load.wait()
     g2 = g_ref[...].reshape(pts, f)
     rows_of = iota((2 * tx, pts), 0)
     want = jnp.where(rows_of < tx, rows_of * ty, (rows_of - tx) * ty + ty - 1)
@@ -99,26 +134,22 @@
         delta = delta.astype(BF16).astype(F32)
         st_own[b] = ln_rows[b * 2 * HEADS:(b + 1) * 2 * HEADS] + delta
 
-    pl.semaphore_wait(barrier, n - 1 + nx - 1)
-
-    big = []
-    targets = [(0, sib)] + [(t, peer(2 * t)) for t in range(1, half)]
-    for t, to in targets[1:] + targets[:1]:
-        at = 1 + t
-        big.append(remote(q_ref, q_in[t], big_send.at[at, 0], big_recv.at[at, 0], mx, to))
-        big.append(remote(g_ref, g_in[t], big_send.at[at, 1], big_recv.at[at, 1], mx, to))
     halo = [
         remote(edge.at[0], yh.at[0], halo_send.at[0], halo_recv.at[0], mx, peer(n - 1)),
         remote(edge.at[1], yh.at[1], halo_send.at[1], halo_recv.at[1], mx, peer(1)),
         remote(g_ref.at[0, pl.ds(0, ty)], xh.at[0], halo_send.at[2], halo_recv.at[2], xpeer(nx - 1), my),
         remote(g_ref.at[rb - 1, pl.ds(BLOCK - ty, ty)], xh.at[1], halo_send.at[3], halo_recv.at[3], xpeer(1), my),
     ]
-    small = []
-    for t in range(1, n):
-        small.append(remote(nb_own, nb_all.at[my], small_send.at[t, 0], small_recv.at[t, 0], mx, peer(t)))
-        small.append(remote(st_own, st_all.at[my], small_send.at[t, 1], small_recv.at[t, 1], mx, peer(t)))
-    for copy in halo + small + big:
+    stats = [
+        remote(st_own, st_all.at[my], small_send.at[t, 1], small_recv.at[t, 1], mx, peer(t))
+        for t in range(1, n)
+    ]
+    for copy in halo + stats:
         copy.start()
+    for t in range(1, half):
+        send_big(t, 1)
+    send_big(0, 0)
+    send_big(0, 1)
 
     def wait_big(number, which):
         ref = (q_in, g_in)[which][number - 1]
@@ -147,6 +178,8 @@
         dqt = dot(kt, jnp.concatenate(grads, 0)) * scale
         return dqt, dk, dv
 
+    for copy in (k_load, v_load, q_load, w_load):
+        copy.wait()
     for b in range(rb):
         k = k_ref[b]
         ktr = k.astype(F32).T.astype(BF16)
@@ -188,8 +221,8 @@
         copy.start()
     col_all[my] = part[...]
 
-    for t in range(1, n):
-        small[2 * (t - 1)].wait_recv()
+    for copy in lists:
+        copy.wait_recv()
     nb_all[my] = nb_own[...]
     to_smem = pltpu.make_async_copy(nb_all, nb_s, local_sem)
     to_smem.start()
@@ -255,8 +288,8 @@
     pass_on(0)
     wait_big(1, 0)
     wait_big(1, 1)
-    for t in range(1, n):
-        small[2 * (t - 1) + 1].wait_recv()
+    for copy in stats:
+        copy.wait_recv()
     work(sib, 1)
     pass_on(1)
 
@@ -294,6 +327,15 @@
         dk_ref[b * BLOCK:(b + 1) * BLOCK] = dk.astype(BF16)
         dv_ref[b * BLOCK:(b + 1) * BLOCK] = dv.astype(BF16)
 
+    stores = [
+        pltpu.make_async_copy(src, dst, store_sem.at[at])
+        for at, (src, dst) in enumerate(
+            [(dk_ref, dk_hbm), (dv_ref, dv_hbm), (sg_ref, sg_hbm), (dq_ref, dq_hbm)]
+        )
+    ]
+    stores[0].start()
+    stores[1].start()
+
     def get_row(t, carry):
         row_copy(t).wait_recv()
         return carry
@@ -301,6 +343,8 @@
     lax.fori_loop(1, nx, get_row, 0)
     total = lax.fori_loop(1, nx, lambda d, acc: acc + row_all[d], row_all[0])
     sg_ref[...] = total / math.sqrt(pts * nx * n)
+
+    stores[2].start()
 
     for copy in returns:
         copy.wait_recv()
@@ -319,7 +363,10 @@
             dqt = dqt + ret_in[place[e] * cap + rank].astype(F32)
         dq_ref[r * BLOCK:(r + 1) * BLOCK] = dqt.T.astype(BF16)
 
-    for copy in halo + small + big + cols + forwards + returns:
+    stores[3].start()
+    for copy in stores:
+        copy.wait()
+    for copy in halo + lists + stats + big + cols + forwards + returns:
         copy.wait_send()
 
     def end_row(t, carry):
@@ -327,6 +374,19 @@
         return carry
 
     lax.fori_loop(1, nx, end_row, 0)
+
+
+def write(dq_ref, dk_ref, dv_ref, sg_ref, dq_hbm, dk_hbm, dv_hbm, sg_hbm, sems):
+    copies = [
+        pltpu.make_async_copy(src, dst, sems.at[at])
+        for at, (src, dst) in enumerate(
+            [(dq_ref, dq_hbm), (dk_ref, dk_hbm), (dv_ref, dv_hbm), (sg_ref, sg_hbm)]
+        )
+    ]
+    for copy in copies:
+        copy.start()
+    for copy in copies:
+        copy.wait()
 
 
 def per_device(nx, n, queries, keys, values, out_attn, out_grad, log_norm, neighbour_blocks, stencil):
@@ -337,15 +397,23 @@
     cap = max(2, (rb * listed + n - 1) // n)
     flat = [a.reshape(rb, BLOCK, f) for a in (queries, keys, values, out_attn, out_grad)]
     vmem = pl.BlockSpec(memory_space=pltpu.VMEM)
+    hbm = pl.BlockSpec(memory_space=pltpu.HBM)
+    flat_buf = pltpu.VMEM((pts, f), BF16)
+    block_buf = pltpu.VMEM((rb, BLOCK, f), BF16)
     half = n // 2
     dma = pltpu.SemaphoreType.DMA
     grads = jax.ShapeDtypeStruct((pts, f), BF16)
     dq, dk, dv, sg = pl.pallas_call(
         functools.partial(kernel, nx, n, tx, ty, rb, listed, cap),
         out_shape=[grads, grads, grads, jax.ShapeDtypeStruct((8, f), F32)],
-        in_specs=[vmem] * 8,
-        out_specs=[vmem] * 4,
+        in_specs=[hbm] * 7 + [vmem],
+        out_specs=[hbm] * 4,
         scratch_shapes=[
+            flat_buf, flat_buf, flat_buf, pltpu.VMEM((8, f), F32), dma((4,)),
+            block_buf, block_buf, block_buf, block_buf, block_buf,
+            pltpu.VMEM(log_norm.shape, BF16),
+            pltpu.VMEM(stencil.shape, F32),
+            dma((7,)),
             [pltpu.VMEM((rb, BLOCK, f), BF16)] * (n - 1),
             [pltpu.VMEM((rb, BLOCK, f), BF16)] * (n - 1),
             pltpu.VMEM((rb, 2 * HEADS, BLOCK), F32),
@@ -377,9 +445,17 @@
             dma,
         ],
         compiler_params=pltpu.CompilerParams(
-            collective_id=0, has_side_effects=True, vmem_limit_bytes=40 * 1024 * 1024
+            collective_id=0, has_side_effects=True, vmem_limit_bytes=56 * 1024 * 1024
         ),
-    )(*flat, log_norm, neighbour_blocks, stencil)
+    )(*flat, log_norm, stencil, neighbour_blocks)
+    dq, dk, dv, sg = pl.pallas_call(
+        write,
+        out_shape=[grads, grads, grads, jax.ShapeDtypeStruct((8, f), F32)],
+        in_specs=[hbm] * 4,
+        out_specs=[hbm] * 4,
+        scratch_shapes=[dma((4,))],
+        compiler_params=pltpu.CompilerParams(vmem_limit_bytes=56 * 1024 * 1024),
+    )(dq, dk, dv, sg)
     shape = (tx, ty, f)
     return dq.reshape(shape), dk.reshape(shape), dv.reshape(shape), sg[:5]
 

time: 31.1 us -> 39.7 us (1.28)
  Pallas kernels: 21.6 us -> 37.5 us
  local copies, waits for them, and re-layouts: 8.56 us -> 1.34 us
    pallas_call x0 -> x1, Pallas kernels: none -> 13.2 us  [per_device(): pl.pallas_call(write, out_shape=[grads, grads, grads, jax.ShapeDtypeStruc...]
    unnamed x21 -> x3, local copies, waits for them, and re-layouts: 8.56 us -> 1.34 us
    pallas_call x1, Pallas kernels: 21.6 us -> 24.4 us  [per_device(): pl.pallas_call(functools.partial(kernel, nx, n, tx, ty, rb, listed, cap),...]
where the time goes in v2:
time: 39.7 us; the launch traced here: 39.5 us
  Pallas kernels  37.5 us (94%)
  local copies, waits for them, and re-layouts  1.34 us (3%)
  between operations  0.65 us (2%)
    pallas_call x1, Pallas kernels, per_device(): pl.pallas_call(functools.partial(kernel, nx, n, tx, ty, rb, listed, cap),...  24.4 us
    pallas_call x1, Pallas kernels, per_device(): pl.pallas_call(write, out_shape=[grads, grads, grads, jax.ShapeDtypeStruc...  13.2 us
    unnamed x3, local copies, waits for them, and re-layouts  1.34 us

profile of v2, /device:TPU:0, one launch (start us, length us, event | category | flops | bytes accessed | tf_op | source)
XLA Modules:
  0.0 39.5 jit_solution(1835103110659040407)
XLA Ops:
  0.6 0.0 copy-start
  0.6 0.7 %copy-done = s32[1,4,3]{1,0,2:T(1,128)S(1)} copy-done((s32[1,4,3]{1,0,2:T(1,128)S(1)}, s32[1,4,3]{1,0,2:T(1,128)}, u32[]{:S(2)}) %copy-start) | copy-done | bytes 72
  1.3 0.7 %copy.12.nb_ref = s32[1,4,3]{2,1,0:T(4,128)} copy(s32[1,4,3]{1,0,2:T(1,128)S(1)} %copy-done) | data formatting | bytes 96 | tf_op args[6]
  2.0 24.4 %shard_map.111 = (bf16[512,128]{1,0:T(8,128)(2,1)}, bf16[512,128]{1,0:T(8,128)(2,1)}, bf16[512,128]{1,0:T(8,128)(2,1)}, f32[8,128]{1,0:T(8,128)}) custom-call(bf16[4,128,128]{2,1,0:T(8,128)(2,1)} %bitcast.9, bf16[4,128,128]{2,1,0:T(8,128)(2,1)} %bitcast.10, bf16[4,128,128]{2,1,0:T(8,128)(2,1)} %bitcast.11, bf16[4,128,128]{2,1,0:T(8,128)(2,1)} %bitcast.12, ...), custom_call_target="tpu_custom_call" | custom-call | tf_op jit(solution)/shard_map/pallas_call | solution.py:406
  26.3 13.2 %shard_map.112 = (bf16[512,128]{1,0:T(8,128)(2,1)}, bf16[512,128]{1,0:T(8,128)(2,1)}, bf16[512,128]{1,0:T(8,128)(2,1)}, f32[8,128]{1,0:T(8,128)}) custom-call(bf16[512,128]{1,0:T(8,128)(2,1)} %get-tuple-element.12.dq_ref, bf16[512,128]{1,0:T(8,128)(2,1)} %get-tuple-element.13.dk_ref, bf16[512,128]{1,0:T(8,128)(2,1)} %get-tuple-element.14.dv_ref, ...), custom_call_target="tpu_custom_call" | custom-call | tf_op jit(solution)/shard_map/pallas_call | solution.py:451
Async XLA Ops:
  0.6 0.7 %copy-start = (s32[1,4,3]{1,0,2:T(1,128)S(1)}, s32[1,4,3]{1,0,2:T(1,128)}, u32[]{:S(2)}) copy-start(s32[1,4,3]{1,0,2:T(1,128)} %param.14) | copy-start | bytes 148

commit v3 on v2

--- a/solution.py
+++ b/solution.py
@@ -29,20 +29,20 @@
 
 def kernel(
     nx, n, tx, ty, rb, listed, cap,
-    q_hbm, k_hbm, v_hbm, o_hbm, g_hbm, ln_hbm, w_hbm, nb_ref,
+    q_hbm, k_hbm, v_hbm, o_hbm, g_hbm, ln_hbm, w_hbm, nb_hbm,
     dq_hbm, dk_hbm, dv_hbm, sg_hbm,
     dq_ref, dk_ref, dv_ref, sg_ref, store_sem,
-    q_ref, k_ref, v_ref, o_ref, g_ref, ln_ref, w_ref, load_sem,
+    q_ref, k_ref, v_ref, o_ref, g_ref, ln_ref, w_ref, nb_ref, load_sem,
     q_in, g_in, st_own, st_all, nb_all, nb_own, nb_s, kmt, edge, xh, yh,
     dq_acc, dk_acc, dv_acc, dk_part, dv_part, ret_out, ret_in,
     part, col_all, row_sum, row_all,
     big_send, big_recv, small_send, small_recv, halo_send, halo_recv,
     ret_send, ret_recv, col_send, col_recv, row_send, row_recv, local_sem,
 ):
-    g_load, o_load, ln_load, k_load, v_load, q_load, w_load = [
+    nb_load, g_load, o_load, ln_load, k_load, v_load, q_load, w_load = [
         pltpu.make_async_copy(src, dst, load_sem.at[at])
         for at, (src, dst) in enumerate([
-            (g_hbm, g_ref), (o_hbm, o_ref), (ln_hbm, ln_ref), (k_hbm, k_ref),
+            (nb_hbm, nb_ref), (g_hbm, g_ref), (o_hbm, o_ref), (ln_hbm, ln_ref), (k_hbm, k_ref),
             (v_hbm, v_ref), (q_hbm, q_ref), (w_hbm, w_ref),
         ])
     ]
@@ -77,10 +77,11 @@
             device_id=(x, y), device_id_type=pl.DeviceIdType.MESH,
         )
 
-    for copy in (g_load, o_load, ln_load, k_load, v_load, q_load, w_load):
+    for copy in (nb_load, g_load, o_load, ln_load, k_load, v_load, q_load, w_load):
         copy.start()
     nb_own[...] = jnp.zeros_like(nb_own)
-    nb_own[0:rb, 0:listed] = nb_ref[0]
+    nb_load.wait()
+    nb_own[0:listed, 0:rb] = nb_ref[...].reshape(listed, rb)
     pl.semaphore_wait(barrier, n - 1 + nx - 1)
 
     lists = [
@@ -234,7 +235,7 @@
         count = jnp.int32(0)
         for r in range(rb):
             for j in range(listed):
-                value = nb_s[src, r, j]
+                value = nb_s[src, j, r]
                 mine = lax.div(value, rb) == my
                 for c in range(cap):
                     here = mine & (count == c)
@@ -351,7 +352,7 @@
     place = []
     for r in range(rb):
         for j in range(listed):
-            value = nb_s[my, r, j]
+            value = nb_s[my, j, r]
             place.append(lax.div(value, rb))
     for r in range(rb):
         dqt = dq_acc[r]
@@ -376,16 +377,23 @@
     lax.fori_loop(1, nx, end_row, 0)
 
 
-def write(dq_ref, dk_ref, dv_ref, sg_ref, dq_hbm, dk_hbm, dv_hbm, sg_hbm, sems):
-    copies = [
-        pltpu.make_async_copy(src, dst, sems.at[at])
-        for at, (src, dst) in enumerate(
-            [(dq_ref, dq_hbm), (dk_ref, dk_hbm), (dv_ref, dv_hbm), (sg_ref, sg_hbm)]
-        )
-    ]
-    for copy in copies:
+def write(dq_in, dk_in, dv_in, sg_in, dq_hbm, dk_hbm, dv_hbm, sg_hbm, dq, dk, dv, sg, sems):
+    loads, stores = [
+        [
+            pltpu.make_async_copy(src, dst, sems.at[way, at])
+            for at, (src, dst) in enumerate(pairs)
+        ]
+        for way, pairs in enumerate([
+            [(dk_in, dk), (dv_in, dv), (dq_in, dq), (sg_in, sg)],
+            [(dk, dk_hbm), (dv, dv_hbm), (dq, dq_hbm), (sg, sg_hbm)],
+        ])
+    ]
+    for copy in loads:
         copy.start()
-    for copy in copies:
+    for load, store in zip(loads, stores):
+        load.wait()
+        store.start()
+    for copy in stores:
         copy.wait()
 
 
@@ -396,7 +404,6 @@
     listed = neighbour_blocks.shape[2]
     cap = max(2, (rb * listed + n - 1) // n)
     flat = [a.reshape(rb, BLOCK, f) for a in (queries, keys, values, out_attn, out_grad)]
-    vmem = pl.BlockSpec(memory_space=pltpu.VMEM)
     hbm = pl.BlockSpec(memory_space=pltpu.HBM)
     flat_buf = pltpu.VMEM((pts, f), BF16)
     block_buf = pltpu.VMEM((rb, BLOCK, f), BF16)
@@ -406,14 +413,15 @@
     dq, dk, dv, sg = pl.pallas_call(
         functools.partial(kernel, nx, n, tx, ty, rb, listed, cap),
         out_shape=[grads, grads, grads, jax.ShapeDtypeStruct((8, f), F32)],
-        in_specs=[hbm] * 7 + [vmem],
+        in_specs=[hbm] * 8,
         out_specs=[hbm] * 4,
         scratch_shapes=[
             flat_buf, flat_buf, flat_buf, pltpu.VMEM((8, f), F32), dma((4,)),
             block_buf, block_buf, block_buf, block_buf, block_buf,
             pltpu.VMEM(log_norm.shape, BF16),
             pltpu.VMEM(stencil.shape, F32),
-            dma((7,)),
+            pltpu.VMEM((listed, 1, rb), jnp.int32),
+            dma((8,)),
             [pltpu.VMEM((rb, BLOCK, f), BF16)] * (n - 1),
             [pltpu.VMEM((rb, BLOCK, f), BF16)] * (n - 1),
             pltpu.VMEM((rb, 2 * HEADS, BLOCK), F32),
@@ -447,13 +455,13 @@
         compiler_params=pltpu.CompilerParams(
             collective_id=0, has_side_effects=True, vmem_limit_bytes=56 * 1024 * 1024
         ),
-    )(*flat, log_norm, stencil, neighbour_blocks)
+    )(*flat, log_norm, stencil, neighbour_blocks.transpose(2, 0, 1))
     dq, dk, dv, sg = pl.pallas_call(
         write,
         out_shape=[grads, grads, grads, jax.ShapeDtypeStruct((8, f), F32)],
         in_specs=[hbm] * 4,
         out_specs=[hbm] * 4,
-        scratch_shapes=[dma((4,))],
+        scratch_shapes=[flat_buf, flat_buf, flat_buf, pltpu.VMEM((8, f), F32), dma((2, 4))],
         compiler_params=pltpu.CompilerParams(vmem_limit_bytes=56 * 1024 * 1024),
     )(dq, dk, dv, sg)
     shape = (tx, ty, f)

time: 39.7 us -> 26.3 us (0.66)
  Pallas kernels: 37.5 us -> 25.5 us
  local copies, waits for them, and re-layouts: 1.34 us -> 0 us
    pallas_call x1, Pallas kernels: 13.2 us -> 1.76 us  [per_device(): pl.pallas_call(write, out_shape=[grads, grads, grads, jax.ShapeDtypeStruc...]
    unnamed x3 -> x0, local copies, waits for them, and re-layouts: 1.34 us -> none
    pallas_call x1, Pallas kernels: 24.4 us -> 23.7 us  [per_device(): pl.pallas_call(functools.partial(kernel, nx, n, tx, ty, rb, listed, cap),...]
where the time goes in v3:
time: 26.3 us; the launch traced here: 26.1 us
  Pallas kernels  25.5 us (97%)
  between operations  0.64 us (2%)
    pallas_call x1, Pallas kernels, per_device(): pl.pallas_call(functools.partial(kernel, nx, n, tx, ty, rb, listed, cap),...  23.7 us
    pallas_call x1, Pallas kernels, per_device(): pl.pallas_call(write, out_shape=[grads, grads, grads, jax.ShapeDtypeStruc...  1.76 us

profile of v3, /device:TPU:0, one launch (start us, length us, event | category | flops | bytes accessed | tf_op | source)
XLA Modules:
  0.0 26.1 jit_solution(4165095862592752140)
XLA Ops:
  0.6 23.7 %shard_map.111 = (bf16[512,128]{1,0:T(8,128)(2,1)}, bf16[512,128]{1,0:T(8,128)(2,1)}, bf16[512,128]{1,0:T(8,128)(2,1)}, f32[8,128]{1,0:T(8,128)}) custom-call(bf16[4,128,128]{2,1,0:T(8,128)(2,1)} %bitcast.10, bf16[4,128,128]{2,1,0:T(8,128)(2,1)} %bitcast.11, bf16[4,128,128]{2,1,0:T(8,128)(2,1)} %bitcast.12, bf16[4,128,128]{2,1,0:T(8,128)(2,1)} %bitcast.13, ...), custom_call_target="tpu_custom_call" | custom-call | tf_op jit(solution)/shard_map/pallas_call | solution.py:413
  24.4 1.8 %shard_map.112 = (bf16[512,128]{1,0:T(8,128)(2,1)}, bf16[512,128]{1,0:T(8,128)(2,1)}, bf16[512,128]{1,0:T(8,128)(2,1)}, f32[8,128]{1,0:T(8,128)}) custom-call(bf16[512,128]{1,0:T(8,128)(2,1)} %get-tuple-element.12.dq_in, bf16[512,128]{1,0:T(8,128)(2,1)} %get-tuple-element.13.dk_in, bf16[512,128]{1,0:T(8,128)(2,1)} %get-tuple-element.14.dv_in, ...), custom_call_target="tpu_custom_call" | custom-call | tf_op jit(solution)/shard_map/pallas_call | solution.py:459

commit v4 on v3

--- a/solution.py
+++ b/solution.py
@@ -30,8 +30,7 @@
 def kernel(
     nx, n, tx, ty, rb, listed, cap,
     q_hbm, k_hbm, v_hbm, o_hbm, g_hbm, ln_hbm, w_hbm, nb_hbm,
-    dq_hbm, dk_hbm, dv_hbm, sg_hbm,
-    dq_ref, dk_ref, dv_ref, sg_ref, store_sem,
+    dq_ref, dk_ref, dv_ref, sg_ref,
     q_ref, k_ref, v_ref, o_ref, g_ref, ln_ref, w_ref, nb_ref, load_sem,
     q_in, g_in, st_own, st_all, nb_all, nb_own, nb_s, kmt, edge, xh, yh,
     dq_acc, dk_acc, dv_acc, dk_part, dv_part, ret_out, ret_in,
@@ -328,15 +327,6 @@
         dk_ref[b * BLOCK:(b + 1) * BLOCK] = dk.astype(BF16)
         dv_ref[b * BLOCK:(b + 1) * BLOCK] = dv.astype(BF16)
 
-    stores = [
-        pltpu.make_async_copy(src, dst, store_sem.at[at])
-        for at, (src, dst) in enumerate(
-            [(dk_ref, dk_hbm), (dv_ref, dv_hbm), (sg_ref, sg_hbm), (dq_ref, dq_hbm)]
-        )
-    ]
-    stores[0].start()
-    stores[1].start()
-
     def get_row(t, carry):
         row_copy(t).wait_recv()
         return carry
@@ -344,8 +334,6 @@
     lax.fori_loop(1, nx, get_row, 0)
     total = lax.fori_loop(1, nx, lambda d, acc: acc + row_all[d], row_all[0])
     sg_ref[...] = total / math.sqrt(pts * nx * n)
-
-    stores[2].start()
 
     for copy in returns:
         copy.wait_recv()
@@ -364,9 +352,6 @@
             dqt = dqt + ret_in[place[e] * cap + rank].astype(F32)
         dq_ref[r * BLOCK:(r + 1) * BLOCK] = dqt.T.astype(BF16)
 
-    stores[3].start()
-    for copy in stores:
-        copy.wait()
     for copy in halo + lists + stats + big + cols + forwards + returns:
         copy.wait_send()
 
@@ -377,23 +362,16 @@
     lax.fori_loop(1, nx, end_row, 0)
 
 
-def write(dq_in, dk_in, dv_in, sg_in, dq_hbm, dk_hbm, dv_hbm, sg_hbm, dq, dk, dv, sg, sems):
-    loads, stores = [
-        [
-            pltpu.make_async_copy(src, dst, sems.at[way, at])
-            for at, (src, dst) in enumerate(pairs)
-        ]
-        for way, pairs in enumerate([
-            [(dk_in, dk), (dv_in, dv), (dq_in, dq), (sg_in, sg)],
-            [(dk, dk_hbm), (dv, dv_hbm), (dq, dq_hbm), (sg, sg_hbm)],
-        ])
-    ]
-    for copy in loads:
+def write(dq, dk, dv, sg, dq_hbm, dk_hbm, dv_hbm, sg_hbm, sems):
+    copies = [
+        pltpu.make_async_copy(src, dst, sems.at[at])
+        for at, (src, dst) in enumerate(
+            [(dq, dq_hbm), (dk, dk_hbm), (dv, dv_hbm), (sg, sg_hbm)]
+        )
+    ]
+    for copy in copies:
         copy.start()
-    for load, store in zip(loads, stores):
-        load.wait()
-        store.start()
-    for copy in stores:
+    for copy in copies:
         copy.wait()
 
 
@@ -405,18 +383,17 @@
     cap = max(2, (rb * listed + n - 1) // n)
     flat = [a.reshape(rb, BLOCK, f) for a in (queries, keys, values, out_attn, out_grad)]
     hbm = pl.BlockSpec(memory_space=pltpu.HBM)
-    flat_buf = pltpu.VMEM((pts, f), BF16)
+    vmem = pl.BlockSpec(memory_space=pltpu.VMEM)
     block_buf = pltpu.VMEM((rb, BLOCK, f), BF16)
     half = n // 2
     dma = pltpu.SemaphoreType.DMA
     grads = jax.ShapeDtypeStruct((pts, f), BF16)
     dq, dk, dv, sg = pl.pallas_call(
         functools.partial(kernel, nx, n, tx, ty, rb, listed, cap),
-        out_shape=[grads, grads, grads, jax.ShapeDtypeStruct((8, f), F32)],
+        out_shape=[pltpu.VMEM((pts, f), BF16)] * 3 + [pltpu.VMEM((8, f), F32)],
         in_specs=[hbm] * 8,
-        out_specs=[hbm] * 4,
+        out_specs=[vmem] * 4,
         scratch_shapes=[
-            flat_buf, flat_buf, flat_buf, pltpu.VMEM((8, f), F32), dma((4,)),
             block_buf, block_buf, block_buf, block_buf, block_buf,
             pltpu.VMEM(log_norm.shape, BF16),
             pltpu.VMEM(stencil.shape, F32),
@@ -459,10 +436,10 @@
     dq, dk, dv, sg = pl.pallas_call(
         write,
         out_shape=[grads, grads, grads, jax.ShapeDtypeStruct((8, f), F32)],
-        in_specs=[hbm] * 4,
+        in_specs=[vmem] * 4,
         out_specs=[hbm] * 4,
-        scratch_shapes=[flat_buf, flat_buf, flat_buf, pltpu.VMEM((8, f), F32), dma((2, 4))],
-        compiler_params=pltpu.CompilerParams(vmem_limit_bytes=56 * 1024 * 1024),
+        scratch_shapes=[dma((4,))],
+        compiler_params=pltpu.CompilerParams(vmem_limit_bytes=4 * 1024 * 1024),
     )(dq, dk, dv, sg)
     shape = (tx, ty, f)
     return dq.reshape(shape), dk.reshape(shape), dv.reshape(shape), sg[:5]

time: 26.3 us -> 24.7 us (0.939)
  Pallas kernels: 25.5 us -> 23.9 us
    pallas_call x1, Pallas kernels: 1.76 us -> 0.78 us  [per_device(): pl.pallas_call(write, out_shape=[grads, grads, grads, jax.ShapeDtypeStruc...]
    pallas_call x1, Pallas kernels: 23.7 us -> 23.1 us  [per_device(): pl.pallas_call(functools.partial(kernel, nx, n, tx, ty, rb, listed, cap),...]
where the time goes in v4:
time: 24.7 us; the launch traced here: 24.5 us
  Pallas kernels  23.9 us (97%)
  between operations  0.64 us (3%)
    pallas_call x1, Pallas kernels, per_device(): pl.pallas_call(functools.partial(kernel, nx, n, tx, ty, rb, listed, cap),...  23.1 us
    pallas_call x1, Pallas kernels, per_device(): pl.pallas_call(write, out_shape=[grads, grads, grads, jax.ShapeDtypeStruc...  0.78 us

profile of v4, /device:TPU:0, one launch (start us, length us, event | category | flops | bytes accessed | tf_op | source)
XLA Modules:
  0.0 24.5 jit_solution(14511573031780261389)
XLA Ops:
  0.6 23.1 %shard_map.111 = (bf16[512,128]{1,0:T(8,128)(2,1)S(1)}, bf16[512,128]{1,0:T(8,128)(2,1)S(1)}, bf16[512,128]{1,0:T(8,128)(2,1)S(1)}, f32[8,128]{1,0:T(8,128)S(1)}) custom-call(bf16[4,128,128]{2,1,0:T(8,128)(2,1)} %bitcast.10, bf16[4,128,128]{2,1,0:T(8,128)(2,1)} %bitcast.11, bf16[4,128,128]{2,1,0:T(8,128)(2,1)} %bitcast.12, bf16[4,128,128]{2,1,0:T(8,128)(2,1)} %bitcast.13, ...), custom_call_target="tpu_custom_call" | custom-call | tf_op jit(solution)/shard_map/pallas_call | solution.py:391
  23.7 0.8 %shard_map.112 = (bf16[512,128]{1,0:T(8,128)(2,1)}, bf16[512,128]{1,0:T(8,128)(2,1)}, bf16[512,128]{1,0:T(8,128)(2,1)}, f32[8,128]{1,0:T(8,128)}) custom-call(bf16[512,128]{1,0:T(8,128)(2,1)S(1)} %get-tuple-element.12.dq, bf16[512,128]{1,0:T(8,128)(2,1)S(1)} %get-tuple-element.13.dk, bf16[512,128]{1,0:T(8,128)(2,1)S(1)} %get-tuple-element.14.dv, ...), custom_call_target="tpu_custom_call" | custom-call | tf_op jit(solution)/shard_map/pallas_call | solution.py:436

commit v5 on v4

--- a/solution.py
+++ b/solution.py
@@ -99,8 +99,9 @@
 
     for copy in lists:
         copy.start()
-    for t in range(1, half):
-        send_big(t, 0)
+    for which in range(2):
+        for t in range(1, half):
+            send_big(t, which)
 
     g_load.wait()
     o_load.wait()
@@ -146,8 +147,6 @@
     ]
     for copy in halo + stats:
         copy.start()
-    for t in range(1, half):
-        send_big(t, 1)
     send_big(0, 0)
     send_big(0, 1)
 

time: 24.7 us -> 26.8 us (1.085)
  Pallas kernels: 23.9 us -> 26 us
    pallas_call x1, Pallas kernels: 23.1 us -> 25.2 us  [per_device(): pl.pallas_call(functools.partial(kernel, nx, n, tx, ty, rb, listed, cap),...]
where the time goes in v5:
time: 26.8 us; the launch traced here: 26.7 us
  Pallas kernels  26 us (97%)
  between operations  0.64 us (2%)
    pallas_call x1, Pallas kernels, per_device(): pl.pallas_call(functools.partial(kernel, nx, n, tx, ty, rb, listed, cap),...  25.2 us
    pallas_call x1, Pallas kernels, per_device(): pl.pallas_call(write, out_shape=[grads, grads, grads, jax.ShapeDtypeStruc...  0.78 us

profile of v5, /device:TPU:0, one launch (start us, length us, event | category | flops | bytes accessed | tf_op | source)
XLA Modules:
  0.0 26.7 jit_solution(565457937936372016)
XLA Ops:
  0.6 25.2 %shard_map.111 = (bf16[512,128]{1,0:T(8,128)(2,1)S(1)}, bf16[512,128]{1,0:T(8,128)(2,1)S(1)}, bf16[512,128]{1,0:T(8,128)(2,1)S(1)}, f32[8,128]{1,0:T(8,128)S(1)}) custom-call(bf16[4,128,128]{2,1,0:T(8,128)(2,1)} %bitcast.10, bf16[4,128,128]{2,1,0:T(8,128)(2,1)} %bitcast.11, bf16[4,128,128]{2,1,0:T(8,128)(2,1)} %bitcast.12, bf16[4,128,128]{2,1,0:T(8,128)(2,1)} %bitcast.13, ...), custom_call_target="tpu_custom_call" | custom-call | tf_op jit(solution)/shard_map/pallas_call | solution.py:390
  25.9 0.8 %shard_map.112 = (bf16[512,128]{1,0:T(8,128)(2,1)}, bf16[512,128]{1,0:T(8,128)(2,1)}, bf16[512,128]{1,0:T(8,128)(2,1)}, f32[8,128]{1,0:T(8,128)}) custom-call(bf16[512,128]{1,0:T(8,128)(2,1)S(1)} %get-tuple-element.12.dq, bf16[512,128]{1,0:T(8,128)(2,1)S(1)} %get-tuple-element.13.dk, bf16[512,128]{1,0:T(8,128)(2,1)S(1)} %get-tuple-element.14.dv, ...), custom_call_target="tpu_custom_call" | custom-call | tf_op jit(solution)/shard_map/pallas_call | solution.py:435
